TPU v7x, 32 devices: a whole 2x2x4 slice. The times are simulated.
32 devices in a mesh: row: 8 (over y, x, core), col: 4 (over z).
Axes of the slice: x: 2, y: 2, z: 4, core: 2. Of those that a mesh axis runs over, the one named last changes fastest.
Arguments:
- block_out: bfloat16 [384, 8192], P('row', 'col'), may hold values from -250 to 250
- stream_mid: bfloat16 [384, 8192], P('row', 'col'), may hold values from -250 to 250
- gate_pre: bfloat16 [384, 28672], P('row', 'col'), may hold values from -8 to 8
- up_pre: bfloat16 [384, 28672], P('row', 'col'), may hold values from -6 to 6
- final_gain: float32 [8192], P('col'), may hold values from 0.28 to 1.72
- mlp_gain: float32 [8192], P('col'), may hold values from 0.1 to 1.9
- value_weight: float32 [8192], P('col'), may hold values from -0.006629126 to 0.006629126
- returns: float32 [384], P('row'), may hold values from -6 to 6
- response_mask: int32 [384], P('row'), may hold values from 0 to 1, as said below
- w_gate: bfloat16 [8192, 28672], P('row', 'col'), may hold values from -0.0625 to 0.0625
- w_up: bfloat16 [8192, 28672], P('row', 'col'), may hold values from -0.0625 to 0.0625
- w_down: bfloat16 [28672, 8192], P('col', 'row'), may hold values from -0.03125 to 0.03125
Outputs:
- stream_mid_gradient: bfloat16 [384, 8192], P('row', 'col')
- d_w_down: float32 [28672, 8192], P('col', 'row')
Inputs may be any that keep to these rules, and one draw needn't show every extreme that they name: `response_mask`: the last token of the micro-batch is a response token.
All inputs are finite; a program needn't handle non-finite values.
Results may differ from a plain program's by a relative error of at most 0.0075.
Values may be sent and summed in bfloat16 or wider, within the bound.
No kernel may reach another device: no remote copies, remote signals or barrier semaphores. Data moves between devices by JAX's collectives and lax.ppermute only.
A program may use at most 128 MiB of HBM per device.

v0:
```python
import math

import jax
import jax.numpy as jnp
from jax import lax
from jax.sharding import PartitionSpec as P

MODEL_WIDTH = 8192


epsilon = 1e-05


def contract(left, right, left_dim, right_dim):
    return lax.dot_general(
        left, right, (((left_dim,), (right_dim,)), ((), ())), preferred_element_type=jnp.float32
    )


def swiglu_grads(d_hidden, gate_wide, up_wide, sigmoid_gate):
    d_gate = (d_hidden * up_wide * sigmoid_gate * (1.0 + gate_wide * (1.0 - sigmoid_gate))).astype(
        jnp.bfloat16
    )
    d_up = (d_hidden * gate_wide * sigmoid_gate).astype(jnp.bfloat16)
    return (d_gate, d_up)


def local(
    block_out,
    stream_mid,
    gate_pre,
    up_pre,
    final_gain,
    mlp_gain,
    value_weight,
    returns,
    response_mask,
    w_gate,
    w_up,
    w_down,
):
    local_rows = block_out.shape[0]
    total_tokens = local_rows * lax.axis_size("row")
    output_widened = block_out.astype(jnp.float32)
    middle_widened = stream_mid.astype(jnp.float32)
    live = response_mask.astype(jnp.float32)
    value_head = final_gain * value_weight
    count = lax.psum(jnp.sum(live), "row")
    square_out, square_mid, head_sum = lax.psum(
        (
            jnp.sum(output_widened * output_widened, axis=1),
            jnp.sum(middle_widened * middle_widened, axis=1),
            jnp.sum(output_widened * value_head[None, :], axis=1),
        ),
        "col",
    )
    output_inverse_root = lax.rsqrt(square_out / MODEL_WIDTH + epsilon)
    middle_inverse_root = lax.rsqrt(square_mid / MODEL_WIDTH + epsilon)
    value_estimate = output_inverse_root * head_sum
    dvalue = live * (value_estimate - returns) * (total_tokens * math.sqrt(MODEL_WIDTH) / count)
    output_normalized_rows = output_widened * output_inverse_root[:, None]
    adjoint_vector = value_head[None, :] * dvalue[:, None]
    inner_product = dvalue * value_estimate
    output_gradient = (
        output_inverse_root[:, None]
        * (adjoint_vector - output_normalized_rows * (inner_product / MODEL_WIDTH)[:, None])
    ).astype(jnp.bfloat16)
    full_rows = lax.all_gather(output_gradient, "col", axis=1, tiled=True)
    tiles = lax.all_to_all(full_rows, "row", split_axis=1, concat_axis=0, tiled=True)
    gate_wide = gate_pre.astype(jnp.float32)
    up_wide = up_pre.astype(jnp.float32)
    sigmoid_gate = jax.nn.sigmoid(gate_wide)
    hidden_local = (gate_wide * sigmoid_gate * up_wide).astype(jnp.bfloat16)
    grad_rows = tiles
    d_w_down = contract(lax.all_gather(hidden_local, "row", axis=0, tiled=True), grad_rows, 0, 0)
    grad_rows = tiles
    d_hidden = lax.psum_scatter(
        contract(grad_rows, w_down, 1, 1), "row", scatter_dimension=0, tiled=True
    )
    d_gate, d_up = swiglu_grads(d_hidden, gate_wide, up_wide, sigmoid_gate)
    stacked = jnp.stack([d_gate, d_up])
    piece = lax.all_gather(stacked, "row", axis=1, tiled=True)
    normed_part = contract(piece[0], w_gate, 1, 1) + contract(piece[1], w_up, 1, 1)
    spread = lax.all_to_all(normed_part, "row", split_axis=0, concat_axis=1, tiled=True)
    d_normed = lax.psum_scatter(spread, "col", scatter_dimension=1, tiled=True)
    middle_normalized_rows = middle_widened * middle_inverse_root[:, None]
    scaled_rows = d_normed * mlp_gain[None, :]
    middle_inner_product = lax.psum(jnp.sum(scaled_rows * middle_normalized_rows, axis=1), "col")
    stream_mid_gradient = output_gradient.astype(jnp.float32) + middle_inverse_root[:, None] * (
        scaled_rows - middle_normalized_rows * (middle_inner_product / MODEL_WIDTH)[:, None]
    )
    return (stream_mid_gradient.astype(jnp.bfloat16), d_w_down)


def solution(mesh):
    placed = (
        P("row", "col"),
        P("row", "col"),
        P("row", "col"),
        P("row", "col"),
        P("col"),
        P("col"),
        P("col"),
        P("row"),
        P("row"),
        P("row", "col"),
        P("row", "col"),
        P("col", "row"),
    )
    return jax.shard_map(
        local,
        mesh=mesh,
        in_specs=placed,
        out_specs=(P("row", "col"), P("col", "row")),
        check_vma=False,
    )
```

profile of v0, /device:TPU:4, one launch (start us, length us, event | category | flops | bytes accessed | tf_op | source)
XLA Modules:
  0.0 361.6 jit_solution(17051774573639795011)
XLA Ops:
  7.2 1.3 convert_reduce_fusion
  8.5 13.3 %psum.37 = f32[]{:T(128)} all-reduce(f32[]{:T(128)} %convert_reduce_fusion), channel_id=1, replica_groups=mesh['row'=8,'col'=4] {'row'}, use_global_device_ids=true, to_apply=%region_5.0 | all-reduce | flops 1 | bytes 8 | tf_op jit(solution)/shard_map/psum | solution.py:48
  22.4 0.7 mul.124
  23.2 1.3 fusion.23
  24.4 12.0 %all-reduce = (f32[48]{0:T(128)S(1)}, f32[48]{0:T(128)S(1)}, f32[48]{0:T(128)S(1)}) all-reduce(f32[48]{0:T(128)S(1)} %get-tuple-element.3, f32[48]{0:T(128)S(1)} %get-tuple-element.2, f32[48]{0:T(128)S(1)} %get-tuple-element.13), channel_id=1, replica_groups=mesh['row'=8,'col'=4] {'col'}, use_global_device_ids=true, to_apply=%region_3.0 | all-reduce | flops 144 | bytes 1152 | tf_op jit(solution)/shard_map/psum | solution.py:49
  36.4 0.7 multiply_multiply_fusion
  37.1 1.1 fusion.28
  38.2 16.3 %all_gather.9 = bf16[48,8192]{1,0:T(8,128)(2,1)S(1)} all-gather(bf16[48,2048]{1,0:T(8,128)(2,1)S(1)} %fusion.28), channel_id=1, replica_groups=mesh['row'=8,'col'=4] {'col'}, dimensions={1}, use_global_device_ids=true | all-gather | bytes 983040 | tf_op jit(solution)/shard_map/all_gather | solution.py:68
  54.5 15.0 %all_to_all.38 = bf16[48,8,1024]{2,0,1:T(8,128)(2,1)S(1)} all-to-all(bf16[48,8,1024]{2,0,1:T(8,128)(2,1)S(1)} %bitcast.31), channel_id=1, replica_groups=mesh['row'=8,'col'=4] {'row'}, dimensions={1} | all-to-all | bytes 1572864 | tf_op jit(solution)/shard_map/all_to_all | solution.py:69
  69.5 21.7 %fusion.29 = f32[384,7168]{1,0:T(8,128)} fusion(bf16[384,1024]{1,0:T(8,128)(2,1)S(1)} %bitcast.33, bf16[7168,1024]{1,0:T(8,128)(2,1)} %param.23), kind=kOutput, calls=%fused_computation.50 | convolution fusion | flops 5637144576 | bytes 26476544 | tf_op jit(solution)/shard_map/dot_general | solution.py:15
  91.2 82.5 %reduce-scatter.3.cloned.1.call-done = f32[48,7168]{1,0:T(8,128)} async-done(((f32[384,7168]{1,0:T(8,128)}), f32[48,7168]{1,0:T(8,128)}) %reduce-scatter.3.cloned.1.call-update) | async-done | bytes 1376272 | tf_op jit(solution)/shard_map/reduce_scatter | solution.py:77
  173.7 3.0 fusion.14
  176.7 1.2 pad_maximum_fusion
  178.0 0.7 all-gather.5.cloned.1.call-update
  178.7 64.5 %all-gather.3.cloned.1.call-done = bf16[2,384,7168]{2,1,0:T(8,128)(2,1)} async-done(((bf16[2,48,7168]{2,1,0:T(8,128)(2,1)}), bf16[2,384,7168]{2,1,0:T(8,128)(2,1)}) %all-gather.3.cloned.1.call-update) | async-done | bytes 11010064 | tf_op jit(solution)/shard_map/all_gather | solution.py:82
  243.3 10.7 %fusion = f32[384,1024]{1,0:T(8,128)S(1)} fusion(bf16[1024,7168]{1,0:T(8,128)(2,1)} %param.22, bf16[2,384,7168]{2,1,0:T(8,128)(2,1)} %all-gather.3.cloned.1.call-done), kind=kOutput, calls=%fused_computation.1 | convolution fusion | flops 5637144576 | bytes 21757952 | tf_op jit(solution)/shard_map/dot_general | solution.py:15
  254.0 11.0 %fusion.2 = f32[384,1024]{1,0:T(8,128)S(1)} fusion(f32[384,1024]{1,0:T(8,128)S(1)} %fusion, bf16[1024,7168]{1,0:T(8,128)(2,1)} %param.21, bf16[2,384,7168]{2,1,0:T(8,128)(2,1)} %all-gather.3.cloned.1.call-done), kind=kOutput, calls=%fused_computation.10 | convolution fusion | flops 5637537792 | bytes 23330816 | tf_op jit(solution)/shard_map/dot_general | solution.py:15
  265.0 37.9 %all_to_all.39 = f32[8,48,1024]{2,1,0:T(8,128)S(1)} all-to-all(f32[8,48,1024]{2,1,0:T(8,128)S(1)} %bitcast.35), channel_id=1, replica_groups=mesh['row'=8,'col'=4] {'row'}, dimensions={0} | all-to-all | bytes 3145728 | tf_op jit(solution)/shard_map/all_to_all | solution.py:84
  302.8 1.3 copy.21
  304.2 17.0 %fusion.30 = f32[7168,1024]{1,0:T(8,128)} fusion(bf16[384,7168]{1,0:T(8,128)(2,1)} %all-gather.5.cloned.1.call-done, bf16[384,1024]{1,0:T(8,128)(2,1)S(1)} %bitcast.34), kind=kOutput, calls=%fused_computation.51 | convolution fusion | flops 5637144576 | bytes 35651584 | tf_op jit(solution)/shard_map/dot_general | solution.py:15
  321.2 20.9 %reduce-scatter.5.cloned.1.call-done = f32[48,2048]{1,0:T(8,128)} async-done(((f32[48,8192]{1,0:T(8,128)}), f32[48,2048]{1,0:T(8,128)}) %reduce-scatter.5.cloned.1.call-update) | async-done | bytes 393232 | tf_op jit(solution)/shard_map/reduce_scatter | solution.py:85
  342.1 1.2 fusion.17
  343.4 9.7 %psum.39 = f32[48]{0:T(128)S(1)} all-reduce(f32[48]{0:T(128)S(1)} %fusion.17), channel_id=1, replica_groups=mesh['row'=8,'col'=4] {'col'}, use_global_device_ids=true, to_apply=%region_11.0 | all-reduce | flops 48 | bytes 384 | tf_op jit(solution)/shard_map/psum | solution.py:88
  353.1 2.0 fusion.21
  (21 shorter events, 0.3 us)
Async XLA Ops:
  7.2 166.6 %reduce-scatter.3.cloned.1.call-start = ((), (), s32[]{:S(2)}) async-start(), calls=%async_computation.4 | async-start | bytes 12386304 | tf_op jit(solution)/shard_map/reduce_scatter | solution.py:77
  91.2 82.6 %copy-start.2 = (bf16[48,7168]{1,0:T(8,128)(2,1)S(1)}, bf16[48,7168]{1,0:T(8,128)(2,1)}, u32[]{:S(2)}) copy-start(bf16[48,7168]{1,0:T(8,128)(2,1)} %param.14) | copy-start | bytes 2064388
  91.2 82.6 %copy-start.3 = (bf16[48,7168]{1,0:T(8,128)(2,1)S(1)}, bf16[48,7168]{1,0:T(8,128)(2,1)}, u32[]{:S(2)}) copy-start(bf16[48,7168]{1,0:T(8,128)(2,1)} %param.15) | copy-start | bytes 2064388
  91.2 152.1 %all-gather.3.cloned.1.call-start = ((), (), s32[]{:S(2)}) async-start(), calls=%async_computation.5 | async-start | bytes 12386304 | tf_op jit(solution)/shard_map/all_gather | solution.py:82
  178.0 126.2 %all-gather.5.cloned.1.call-start = ((), (), s32[]{:S(2)}) async-start(), calls=%async_computation.7 | async-start | bytes 6193152 | tf_op jit(solution)/shard_map/all_gather | solution.py:75
  178.7 163.4 %reduce-scatter.5.cloned.1.call-start = ((), (), s32[]{:S(2)}) async-start(), calls=%async_computation.6 | async-start | bytes 1966080 | tf_op jit(solution)/shard_map/reduce_scatter | solution.py:85
  304.1 38.0 %copy-start = (bf16[48,2048]{1,0:T(8,128)(2,1)S(1)}, bf16[48,2048]{1,0:T(8,128)(2,1)}, u32[]{:S(2)}) copy-start(bf16[48,2048]{1,0:T(8,128)(2,1)} %param.13) | copy-start | bytes 589828
  304.1 38.0 %copy-start.4 = (f32[2048]{0:T(1024)S(1)}, f32[2048]{0:T(1024)}, u32[]{:S(2)}) copy-start(f32[2048]{0:T(1024)} %param.17) | copy-start | bytes 24580
  304.2 49.0 %copy-start.1 = (bf16[48,2048]{1,0:T(8,128)(2,1)S(1)}, bf16[48,2048]{1,0:T(8,128)(2,1)}, u32[]{:S(2)}) copy-start(bf16[48,2048]{1,0:T(8,128)(2,1)} %param.12) | copy-start | bytes 589828
Sparse Core Ops, SparseCore 0:
  91.3 82.3 reduce-scatter.2
  178.1 65.1 all-gather.2
  245.1 57.2 all-gather.4
  304.6 37.5 reduce-scatter.4
where the time goes:
time: 364 us; the launch traced here: 362 us
  waiting for transfers between devices  169 us (46%)
  blocking collectives  104 us (29%)
  matrix products  60.4 us (17%)
  between operations  14.5 us (4%)
  other arithmetic  12.4 us (3%)
    reduce_scatter x1, waiting for transfers between devices, local(): lax.psum_scatter(contract(grad_rows, w_down, 1, 1), 'row', scatter_dimens...  82.5 us
    all_gather x1, waiting for transfers between devices, local(): piece = lax.all_gather(stacked, 'row', axis=1, tiled=True)  64.5 us
    dot_general x4, matrix products, contract(): lax.dot_general(left, right, (((left_dim,), (right_dim,)), ((), ())), pre...  60.4 us
    all_to_all x1, blocking collectives, local(): lax.all_to_all(normed_part, 'row', split_axis=0, concat_axis=1, tiled=True)  37.9 us
    reduce_scatter x1, waiting for transfers between devices, local(): d_normed = lax.psum_scatter(spread, 'col', scatter_dimension=1, tiled=True)  20.9 us
    all_gather x1, blocking collectives, local(): full_rows = lax.all_gather(output_gradient, 'col', axis=1, tiled=True)  16.3 us
    all_to_all x1, blocking collectives, local(): lax.all_to_all(full_rows, 'row', split_axis=1, concat_axis=0, tiled=True)  15 us
    psum x1, blocking collectives, local(): count = lax.psum(jnp.sum(live), 'row')  13.3 us
  transfers between devices with their start and end apart: 4, of which 3 were waited for; matrix products, arithmetic and copies ran while one was open for 11% of the time, Pallas kernels for 0%

commit v1 on v0

v1 whole, which is shorter than its diff:
```python
import math

import jax
import jax.numpy as jnp
from jax import lax
from jax.sharding import PartitionSpec as P

epsilon = 1e-05


def contract(left, right, left_dim, right_dim):
    return lax.dot_general(
        left, right, (((left_dim,), (right_dim,)), ((), ())), preferred_element_type=jnp.float32
    )


def exchange_pairs(rows, cols):
    k = rows // cols
    steps = []
    for s in range(k):
        pairs = []
        for r in range(rows):
            for c in range(cols):
                target = (k * c + (r + s) % k, r // k)
                pairs.append((r * cols + c, target[0] * cols + target[1]))
        steps.append(pairs)
    return steps


def local(
    block_out,
    stream_mid,
    gate_pre,
    up_pre,
    final_gain,
    mlp_gain,
    value_weight,
    returns,
    response_mask,
    w_gate,
    w_up,
    w_down,
):
    rows, cols = lax.axis_size("row"), lax.axis_size("col")
    row, col = lax.axis_index("row"), lax.axis_index("col")
    k = rows // cols
    both = ("row", "col")
    own, block = block_out.shape
    width = block * cols
    tile = width // rows
    tokens = own * rows
    steps = exchange_pairs(rows, cols)
    lane = row % k

    gate_all = lax.all_gather(gate_pre, "row", axis=0, tiled=True)
    up_all = lax.all_gather(up_pre, "row", axis=0, tiled=True)

    streams = jnp.stack([block_out, stream_mid]).reshape(2, own, k, tile)
    arrived = []
    for s in range(k):
        piece = lax.dynamic_index_in_dim(streams, (lane + s) % k, axis=2, keepdims=False)
        arrived.append(lax.ppermute(piece, both, steps[s]))
    held = jnp.stack(arrived)
    held = jnp.stack(
        [lax.dynamic_index_in_dim(held, (lane - p) % k, axis=0, keepdims=False) for p in range(k)], axis=1
    ).reshape(2, k * own, tile)
    out_tile = lax.all_gather(held[0], "col", axis=0, tiled=True)
    mid_tile = held[1]

    out_wide = block_out.astype(jnp.float32)
    mid_wide = stream_mid.astype(jnp.float32)
    head_local = final_gain * value_weight
    part = block // rows
    small = jnp.concatenate(
        [
            jnp.sum(out_wide * out_wide, axis=1),
            jnp.sum(out_wide * head_local[None, :], axis=1),
            jnp.sum(mid_wide * mid_wide, axis=1),
            returns,
            response_mask.astype(jnp.float32),
            lax.dynamic_slice_in_dim(head_local, row * part, part),
            lax.dynamic_slice_in_dim(mlp_gain, row * part, part),
        ]
    )
    gathered = lax.all_gather(small, both, axis=0, tiled=False).reshape(rows, cols, -1)
    sums = jnp.sum(gathered[:, :, : 3 * own], axis=1).reshape(rows, 3, own)
    square_out, head_sum, square_mid = (sums[:, i].reshape(-1) for i in range(3))
    targets = gathered[:, 0, 3 * own : 4 * own].reshape(-1)
    live = gathered[:, 0, 4 * own : 5 * own].reshape(-1)
    gains = gathered[:, :, 5 * own :].reshape(rows, cols, 2, part)
    gains = gains.transpose(2, 1, 0, 3).reshape(2, rows, tile)
    tile_gains = lax.dynamic_index_in_dim(gains, row, axis=1, keepdims=False)

    count = jnp.sum(live)
    out_root = lax.rsqrt(square_out / width + epsilon)
    mid_root = lax.rsqrt(square_mid / width + epsilon)
    value = out_root * head_sum
    dvalue = live * (value - targets) * (tokens * math.sqrt(width) / count)
    inner = dvalue * value / width

    def output_gradient(rows_of, root, scale, product, head):
        normalized = rows_of.astype(jnp.float32) * root[:, None]
        return (
            root[:, None] * (head[None, :] * scale[:, None] - normalized * product[:, None])
        ).astype(jnp.bfloat16)

    d_out = output_gradient(out_tile, out_root, dvalue, inner, tile_gains[0])

    partial = contract(d_out, w_down, 1, 1).astype(jnp.bfloat16)
    d_hidden = lax.psum(partial, "row").astype(jnp.float32)

    gate = gate_all.astype(jnp.float32)
    up = up_all.astype(jnp.float32)
    sig = jax.nn.sigmoid(gate)
    hidden = (gate * sig * up).astype(jnp.bfloat16)
    d_w_down = contract(hidden, d_out, 0, 0)
    d_gate = (d_hidden * up * sig * (1.0 + gate * (1.0 - sig))).astype(jnp.bfloat16)
    d_up = (d_hidden * gate * sig).astype(jnp.bfloat16)
    normed_part = contract(d_gate, w_gate, 1, 1) + contract(d_up, w_up, 1, 1)

    quarter = lax.psum_scatter(
        normed_part.astype(jnp.bfloat16), "col", scatter_dimension=0, tiled=True
    )
    quarter_root = lax.dynamic_slice_in_dim(mid_root, col * k * own, k * own)
    product_part = jnp.sum(
        quarter.astype(jnp.float32)
        * tile_gains[1][None, :]
        * (mid_tile.astype(jnp.float32) * quarter_root[:, None]),
        axis=1,
    )
    pieces = quarter.reshape(k, own, tile)
    back = []
    for s in range(k):
        piece = lax.dynamic_index_in_dim(pieces, (lane + s) % k, axis=0, keepdims=False)
        back.append(lax.ppermute(piece, both, steps[s]))
    back = jnp.stack(back)
    d_normed = jnp.concatenate(
        [lax.dynamic_index_in_dim(back, (lane - j) % k, axis=0, keepdims=False) for j in range(k)], axis=1
    ).astype(jnp.float32)
    products = lax.all_gather(product_part, both, axis=0, tiled=False).reshape(rows, tokens)
    products = jnp.sum(products, axis=0)

    def mine(values):
        return lax.dynamic_slice_in_dim(values, row * own, own)

    own_root = mine(mid_root)
    own_d_out = output_gradient(block_out, mine(out_root), mine(dvalue), mine(inner), head_local)
    gradient = own_d_out.astype(jnp.float32) + own_root[:, None] * (
        d_normed * mlp_gain[None, :] - mid_wide * own_root[:, None] * (mine(products) / width)[:, None]
    )
    return (gradient.astype(jnp.bfloat16), d_w_down)


def solution(mesh):
    placed = (
        P("row", "col"),
        P("row", "col"),
        P("row", "col"),
        P("row", "col"),
        P("col"),
        P("col"),
        P("col"),
        P("row"),
        P("row"),
        P("row", "col"),
        P("row", "col"),
        P("col", "row"),
    )
    return jax.shard_map(
        local,
        mesh=mesh,
        in_specs=placed,
        out_specs=(P("row", "col"), P("col", "row")),
        check_vma=False,
    )
```

time: 364 us -> 508 us (1.40)
  waiting for transfers between devices: 169 us -> 322 us
  blocking collectives: 104 us -> 59.3 us
  matrix products: 60.4 us -> 82.8 us
  starting transfers between devices: 0.16 us -> 8.85 us
  local copies, waits for them, and re-layouts: 1.34 us -> 9.27 us
  other arithmetic: 12.4 us -> 6.75 us
    unnamed x4 -> x6, waiting for transfers between devices: 0.73 us -> 129 us
    reduce_scatter x2 -> x1, waiting for transfers between devices: 103 us -> 4.32 us  [local(): lax.psum_scatter(normed_part.astype(jnp.bfloat16), 'col', scatter_dimensi...]
    psum x0 -> x1, waiting for transfers between devices: none -> 92.5 us  [local(): d_hidden = lax.psum(partial, 'row').astype(jnp.float32)]
    all_to_all x2 -> x0, blocking collectives: 52.8 us -> none  [the longest x1 37.9 us: local(): lax.all_to_all(normed_part, 'row', split_axis=0, concat_axis=1, tiled=True)]
    unnamed x0 -> x1, blocking collectives: none -> 39.6 us
    psum x3 -> x0, blocking collectives: 35 us -> none  [the longest x1 13.3 us: local(): count = lax.psum(jnp.sum(live), 'row')]
    all_gather x2, waiting for transfers between devices: 64.5 us -> 88.2 us  [the longest x1 44.2 us: local(): gate_all = lax.all_gather(gate_pre, 'row', axis=0, tiled=True)]
    dot_general x4, matrix products: 60.4 us -> 82.8 us  [contract(): lax.dot_general(left, right, (((left_dim,), (right_dim,)), ((), ())), pre...]
  transfers between devices with their start and end apart: 4 -> 9, of which waited for: 3 -> 7; matrix products, arithmetic and copies ran while one was open for 11% -> 5% of each run, Pallas kernels for 0% -> 0%
where the time goes in v1:
time: 508 us; the launch traced here: 504 us
  waiting for transfers between devices  322 us (63%)
  matrix products  82.8 us (16%)
  blocking collectives  59.3 us (12%)
  between operations  14.8 us (3%)
  local copies, waits for them, and re-layouts  9.27 us (2%)
  starting transfers between devices  8.85 us (2%)
  other arithmetic  6.75 us (1%)
    unnamed x6, waiting for transfers between devices  129 us
    psum x1, waiting for transfers between devices, local(): d_hidden = lax.psum(partial, 'row').astype(jnp.float32)  92.5 us
    dot_general x4, matrix products, contract(): lax.dot_general(left, right, (((left_dim,), (right_dim,)), ((), ())), pre...  82.8 us
    all_gather x1, waiting for transfers between devices, local(): gate_all = lax.all_gather(gate_pre, 'row', axis=0, tiled=True)  44.2 us
    all_gather x1, waiting for transfers between devices, local(): up_all = lax.all_gather(up_pre, 'row', axis=0, tiled=True)  44 us
    unnamed x1, blocking collectives  39.6 us
    all_gather x1, blocking collectives, local(): out_tile = lax.all_gather(held[0], 'col', axis=0, tiled=True)  19.8 us
  transfers between devices with their start and end apart: 9, of which 7 were waited for; matrix products, arithmetic and copies ran while one was open for 5% of the time, Pallas kernels for 0%

profile of v1, /device:TPU:4, one launch (start us, length us, event | category | flops | bytes accessed | tf_op | source)
XLA Modules:
  0.0 503.5 jit_solution(7003203445967226891)
XLA Ops:
  7.9 1.1 fusion.19
  10.5 1.1 fusion.26
  13.4 1.1 stack.36
  14.5 1.1 stack.37
  15.9 0.8 constant_dynamic-slice_fusion.1
  16.8 4.4 collective-permute-start
  21.8 127.4 %all-reduce.7.cloned.1.call-done = f32[24064]{0:T(1024)} async-done(((f32[24064]{0:T(1024)}), f32[24064]{0:T(1024)}) %all-reduce.7.cloned.1.call-update) | async-done | bytes 96272
  149.2 1.0 reshape.98
  152.5 19.8 %all_gather.23 = bf16[384,1024]{1,0:T(8,128)(2,1)S(1)} all-gather(bf16[96,1024]{1,0:T(8,128)(2,1)S(1)} %bitcast.37), channel_id=1, replica_groups=mesh['row'=8,'col'=4] {'col'}, dimensions={0}, use_global_device_ids=true | all-gather | bytes 983040 | tf_op jit(solution)/shard_map/all_gather | solution.py:67
  172.3 21.4 %convolution_convert_fusion = bf16[384,7168]{1,0:T(8,128)(2,1)} fusion(bf16[7168,1024]{1,0:T(8,128)(2,1)} %param.23, bf16[384,1024]{1,0:T(8,128)(2,1)S(1)} %all_gather.23, f32[384]{0:T(512)S(1)} %get-tuple-element.10, f32[384]{0:T(512)S(1)} %get-tuple-element.11, f32[1024]{0:T(1024)S(1)} %bitcast.46, f32[384]{0:T(512)S(1)} %rsqrt.23), kind=kOutput, calls=%fused_computation.16 | convolution fusion | flops 5642649600 | bytes 20980224 | tf_op jit(solution)/shard_map/dot_general | solution.py:12
  195.7 92.5 %all-reduce.5.cloned.1.call-done = bf16[384,7168]{1,0:T(8,128)(2,1)} async-done(((bf16[384,7168]{1,0:T(8,128)(2,1)}), bf16[384,7168]{1,0:T(8,128)(2,1)}) %all-reduce.5.cloned.1.call-update) | async-done | bytes 5505040 | tf_op jit(solution)/shard_map/psum | solution.py:110
  288.3 44.2 %all-gather.7.cloned.1.call-done = bf16[384,7168]{1,0:T(8,128)(2,1)} async-done(((bf16[48,7168]{1,0:T(8,128)(2,1)}), bf16[384,7168]{1,0:T(8,128)(2,1)}) %all-gather.7.cloned.1.call-update) | async-done | bytes 5505040 | tf_op jit(solution)/shard_map/all_gather | solution.py:55
  332.5 44.0 %all-gather.5.cloned.1.call-done = bf16[384,7168]{1,0:T(8,128)(2,1)} async-done(((bf16[48,7168]{1,0:T(8,128)(2,1)}), bf16[384,7168]{1,0:T(8,128)(2,1)}) %all-gather.5.cloned.1.call-update) | async-done | bytes 5505040 | tf_op jit(solution)/shard_map/all_gather | solution.py:56
  376.5 24.0 %fusion.15 = f32[384,1024]{1,0:T(8,128)S(1)} fusion(bf16[1024,7168]{1,0:T(8,128)(2,1)} %param.21, bf16[384,7168]{1,0:T(8,128)(2,1)} %all-gather.5.cloned.1.call-done, bf16[384,7168]{1,0:T(8,128)(2,1)} %all-reduce.5.cloned.1.call-done, bf16[384,7168]{1,0:T(8,128)(2,1)} %all-gather.7.cloned.1.call-done), kind=kOutput, calls=%fused_computation.20 | convolution fusion | flops 5672927232 | bytes 32768000 | tf_op jit(solution)/shard_map/dot_general | solution.py:12
  400.5 18.1 %add_convert_fusion = bf16[384,1024]{1,0:T(8,128)(2,1)} fusion(f32[384,1024]{1,0:T(8,128)S(1)} %fusion.15, bf16[1024,7168]{1,0:T(8,128)(2,1)} %param.22, bf16[384,7168]{1,0:T(8,128)(2,1)} %all-gather.7.cloned.1.call-done, bf16[384,7168]{1,0:T(8,128)(2,1)} %all-reduce.5.cloned.1.call-done), kind=kOutput, calls=%fused_computation.21 | convolution fusion | flops 5659951104 | bytes 28049408 | tf_op jit(solution)/shard_map/dot_general | solution.py:12
  418.6 19.3 %fusion.10 = f32[7168,1024]{1,0:T(8,128)} fusion(bf16[384,7168]{1,0:T(8,128)(2,1)} %all-gather.5.cloned.1.call-done, bf16[384,7168]{1,0:T(8,128)(2,1)} %all-gather.7.cloned.1.call-done, bf16[384,1024]{1,0:T(8,128)(2,1)S(1)} %all_gather.23, f32[384]{0:T(512)S(1)} %get-tuple-element.10, f32[384]{0:T(512)S(1)} %get-tuple-element.11, f32[1024]{0:T(1024)S(1)} %bitcast.47, ...), kind=kOutput, calls=%fused_computation.17 | convolution fusion | flops 5661917184 | bytes 41165312 | tf_op jit(solution)/shard_map/dot_general | solution.py:12
  437.9 4.3 reduce-scatter.2.cloned.1.call-done
  442.3 1.1 fusion.32
  443.7 39.6 %all-reduce.1 = f32[3072]{0:T(1024)S(1)} all-reduce(f32[3072]{0:T(1024)S(1)} %dynamic-update-slice.1), channel_id=3, replica_groups=mesh['row'=8,'col'=4] {'row','col'}, use_global_device_ids=true, to_apply=%add.1 | all-reduce | flops 3072 | bytes 24576
  483.3 1.0 dynamic-slice_bitcast_fusion
  484.4 3.4 collective-permute-start.2
  487.9 5.2 %collective-permute-done.3 = bf16[48,1024]{1,0:T(8,128)(2,1)S(1)} collective-permute-done((bf16[48,1024]{1,0:T(8,128)(2,1)S(1)}, bf16[48,1024]{1,0:T(8,128)(2,1)S(1)}, u32[]{:S(2)}, u32[]{:S(2)}) %collective-permute-start.3) | collective-permute-done | bytes 98336 | tf_op jit(solution)/shard_map/ppermute | solution.py:135
  493.1 2.8 collective-permute-done.2
  496.0 1.0 fusion.24
  (60 shorter events, 9.0 us)
Async XLA Ops:
  7.2 142.0 %all-reduce.7.cloned.1.call-start = ((), (), s32[]{:S(2)}) async-start(), calls=%async_computation.5 | async-start | bytes 196608
  12.7 0.6 copy-start.2
  13.3 275.0 %all-reduce.5.cloned.1.call-start = ((), (), s32[]{:S(2)}) async-start(), calls=%async_computation.1 | async-start | bytes 11010048 | tf_op jit(solution)/shard_map/psum | solution.py:110
  16.8 135.5 %collective-permute-start = (bf16[2,48,1024]{2,1,0:T(8,128)(2,1)S(1)}, bf16[2,48,1024]{2,1,0:T(8,128)(2,1)S(1)}, u32[]{:S(2)}, u32[]{:S(2)}) collective-permute-start(bf16[2,48,1024]{2,1,0:T(8,128)(2,1)S(1)} %bitcast.40), channel_id=1, source_target_pairs={{0,0},{1,8},{2,16},{3,24},{4,4},{5,12},{6,20},{7,28},{8,1},{9,9},{... | collective-permute-start | bytes 589832 | tf_op jit(solution)/shard_map/ppermute | solution.py:62
  21.3 131.0 %collective-permute-start.1 = (bf16[2,48,1024]{2,1,0:T(8,128)(2,1)S(1)}, bf16[2,48,1024]{2,1,0:T(8,128)(2,1)S(1)}, u32[]{:S(2)}, u32[]{:S(2)}) collective-permute-start(bf16[2,48,1024]{2,1,0:T(8,128)(2,1)S(1)} %bitcast.42), channel_id=1, source_target_pairs={{0,4},{1,12},{2,20},{3,28},{4,0},{5,8},{6,16},{7,24},{8,5},{9,13},... | collective-permute-start | bytes 589832 | tf_op jit(solution)/shard_map/ppermute | solution.py:62
  193.7 138.7 %all-gather.7.cloned.1.call-start = ((), (), s32[]{:S(2)}) async-start(), calls=%async_computation.3 | async-start | bytes 6193152 | tf_op jit(solution)/shard_map/all_gather | solution.py:55
  194.5 182.0 %all-gather.5.cloned.1.call-start = ((), (), s32[]{:S(2)}) async-start(), calls=%async_computation.2 | async-start | bytes 6193152 | tf_op jit(solution)/shard_map/all_gather | solution.py:56
  195.1 247.2 %reduce-scatter.2.cloned.1.call-start = ((), (), s32[]{:S(2)}) async-start(), calls=%async_computation.4 | async-start | bytes 983040 | tf_op jit(solution)/shard_map/reduce_scatter | solution.py:121
  418.6 77.4 %copy-start = (bf16[48,2048]{1,0:T(8,128)(2,1)S(1)}, bf16[48,2048]{1,0:T(8,128)(2,1)}, u32[]{:S(2)}) copy-start(bf16[48,2048]{1,0:T(8,128)(2,1)} %param.13) | copy-start | bytes 589828
  418.6 77.4 %copy-start.1 = (bf16[48,2048]{1,0:T(8,128)(2,1)S(1)}, bf16[48,2048]{1,0:T(8,128)(2,1)}, u32[]{:S(2)}) copy-start(bf16[48,2048]{1,0:T(8,128)(2,1)} %param.12) | copy-start | bytes 589828
  418.6 77.4 %copy-start.3 = (f32[2048]{0:T(1024)S(1)}, f32[2048]{0:T(1024)}, u32[]{:S(2)}) copy-start(f32[2048]{0:T(1024)} %param.17) | copy-start | bytes 24580
  484.3 8.8 %collective-permute-start.3 = (bf16[48,1024]{1,0:T(8,128)(2,1)S(1)}, bf16[48,1024]{1,0:T(8,128)(2,1)S(1)}, u32[]{:S(2)}, u32[]{:S(2)}) collective-permute-start(bf16[48,1024]{1,0:T(8,128)(2,1)S(1)} %get-tuple-element.20), channel_id=1, source_target_pairs={{0,4},{1,12},{2,20},{3,28},{4,0},{5,8},{6,16},{7,24},{8,5},{9,13},... | collective-permute-start | bytes 294920 | tf_op jit(solution)/shard_map/ppermute | solution.py:135
  484.4 11.5 %collective-permute-start.2 = (bf16[48,1024]{1,0:T(8,128)(2,1)S(1)}, bf16[48,1024]{1,0:T(8,128)(2,1)S(1)}, u32[]{:S(2)}, u32[]{:S(2)}) collective-permute-start(bf16[48,1024]{1,0:T(8,128)(2,1)S(1)} %get-tuple-element.21), channel_id=1, source_target_pairs={{0,0},{1,8},{2,16},{3,24},{4,4},{5,12},{6,20},{7,28},{8,1},{9,9},{... | collective-permute-start | bytes 294920 | tf_op jit(solution)/shard_map/ppermute | solution.py:135
Sparse Core Ops, SparseCore 0:
  14.1 134.9 all-reduce.6
  193.9 94.3 all-reduce.4
  290.2 42.2 all-gather.6
  334.2 42.2 all-gather.4
  418.7 23.5 reduce-scatter.1

commit v2 on v0

v2 whole, which is shorter than its diff:
```python
import functools
import math

import jax
import jax.numpy as jnp
from jax import lax
from jax.experimental import pallas as pl
from jax.experimental.pallas import tpu as pltpu
from jax.sharding import PartitionSpec as P

epsilon = 1e-05
LANES = 128
MIB = 1024 * 1024
F32 = jnp.float32
BF16 = jnp.bfloat16


def bits_of(n):
    return [1 << i for i in range(n.bit_length() - 1)]


def block_of(extent, most):
    best = LANES
    for size in range(LANES, most + 1, LANES):
        if extent % size == 0:
            best = size
    return best


def call(kernel, grid, ins, outs, shapes, scratch=(), limit=40, cost=None, aliases={}):
    return pl.pallas_call(
        kernel,
        grid=grid,
        in_specs=ins,
        out_specs=outs,
        out_shape=shapes,
        scratch_shapes=list(scratch),
        input_output_aliases=aliases,
        compiler_params=pltpu.CompilerParams(
            dimension_semantics=("arbitrary",) * len(grid), vmem_limit_bytes=limit * MIB
        ),
        cost_estimate=cost,
    )


def cost(flops, moved, special=0):
    return pl.CostEstimate(flops=int(flops), bytes_accessed=int(moved), transcendentals=int(special))


def whole(shape):
    return pl.BlockSpec(shape, lambda i: (0,) * len(shape))


def column(values, position):
    return values[:, position : position + 1]


def place(columns, rows):
    lane = lax.broadcasted_iota(jnp.int32, (rows, LANES), 1)
    out = jnp.zeros((rows, LANES), F32)
    for position, values in enumerate(columns):
        out = jnp.where(lane == position, values, out)
    return out


def sums_kernel(out_ref, mid_ref, gain_ref, weight_ref, sums_ref, head_ref):
    wide = out_ref[...].astype(F32)
    mid = mid_ref[...].astype(F32)
    head = gain_ref[...] * weight_ref[...]
    head_ref[...] = head
    sums_ref[...] = place(
        [
            jnp.sum(wide * wide, axis=1, keepdims=True),
            jnp.sum(wide * head, axis=1, keepdims=True),
            jnp.sum(mid * mid, axis=1, keepdims=True),
        ],
        out_ref.shape[0],
    )


def token_kernel(width, *refs):
    *parts, returns_ref, live_ref, token_ref = refs
    total = parts[0][...]
    for part in parts[1:]:
        total = total + part[...]
    root = lax.rsqrt(column(total, 0) / width + epsilon)
    mid_root = lax.rsqrt(column(total, 2) / width + epsilon)
    value = root * column(total, 1)
    live = live_ref[...].astype(F32)
    token_ref[...] = place(
        [root, value, live * (value - returns_ref[...]), live, mid_root], total.shape[0]
    )


def gradient_rows(rows_of, token, factor, width, head):
    root = column(token, 0)
    dvalue = column(token, 2) * factor
    product = dvalue * column(token, 1) / width
    normalized = rows_of * root
    return (root * (head * dvalue - normalized * product)).astype(BF16)


def out_kernel(width, rows, k, own, shift_ref, head_ref, *refs):
    tokens, pieces, (d_out_ref, factor_ref) = refs[:rows], refs[rows:-2], refs[-2:]
    held = jnp.concatenate([ref[...] for ref in tokens], axis=0)
    count = jnp.sum(column(held, 3), axis=0, keepdims=True)
    factor = (len(tokens) * own * math.sqrt(width)) / count
    factor_ref[...] = jnp.broadcast_to(factor, factor_ref.shape)
    head = head_ref[...]
    for d, piece in enumerate(pieces):
        at = lax.bitwise_xor(shift_ref[0], d)
        for s in range(k):
            rows_of = piece[s].astype(F32)
            token = tokens[0][...]
            for q in range(len(tokens)):
                token = jnp.where(at * k + s == q, tokens[q][...], token)
            d_out_ref[at * k + s] = gradient_rows(rows_of, token, factor, width, head)


def partial_kernel(d_out_ref, w_ref, send_ref, keep_ref):
    count, own, tile = d_out_ref.shape
    result = lax.dot_general(
        d_out_ref[...].reshape(count * own, tile),
        w_ref[...],
        (((1,), (1,)), ((), ())),
        preferred_element_type=F32,
    ).astype(BF16)
    result = result.reshape(count, own, -1)
    for q in range(count):
        (send_ref if q % 2 else keep_ref)[q // 2] = result[q]


def add_kernel(bit, keep_ref, came_ref, *outs):
    sent = kept = 0
    for q in range(keep_ref.shape[0]):
        total = (keep_ref[q].astype(F32) + came_ref[q].astype(F32)).astype(BF16)
        if len(outs) == 1:
            outs[0][...] = total
        elif q & bit:
            outs[0][sent] = total
            sent += 1
        else:
            outs[1][kept] = total
            kept += 1


def add(keep, came, bit):
    count, own, extent = keep.shape
    fb = block_of(extent, 1024)
    block = pl.BlockSpec((count, own, fb), lambda i: (0, 0, i))
    half = count // 2
    if count == 1:
        outs = [pl.BlockSpec((own, fb), lambda i: (0, i))]
        shapes = [jax.ShapeDtypeStruct((own, extent), BF16)]
    else:
        outs = [pl.BlockSpec((half, own, fb), lambda i: (0, 0, i))] * 2
        shapes = [jax.ShapeDtypeStruct((half, own, extent), BF16)] * 2
    return call(
        functools.partial(add_kernel, bit),
        (extent // fb,),
        [block, block],
        outs,
        shapes,
        cost=cost(count * own * extent, 6 * count * own * extent),
    )(keep, came)


def weight_kernel(d_out_ref, *refs):
    pieces, out_ref = refs[: d_out_ref.shape[0]], refs[-1]
    count, own, tile = d_out_ref.shape
    hidden = []
    for piece in pieces:
        gate, up = piece[0].astype(F32), piece[1].astype(F32)
        hidden.append((gate * jax.nn.sigmoid(gate) * up).astype(BF16))
    hidden = jnp.concatenate(hidden, axis=0)
    out_ref[...] = lax.dot_general(
        hidden,
        d_out_ref[...].reshape(count * own, tile),
        (((0,), (0,)), ((), ())),
        preferred_element_type=F32,
    )


def normed_kernel(first, last, k, shift_ref, w_gate_ref, w_up_ref, *refs):
    total = refs[-1]
    out_ref = refs[-2]
    refs = list(refs[:-2])
    before = None if first else refs.pop()
    count = len(refs) // 2
    pieces, grads = refs[:count], refs[count:]
    own = grads[0].shape[0]
    step = pl.program_id(0)

    d_gates, d_ups = [], []
    for piece, grad in zip(pieces, grads):
        gate, up, d_hidden = piece[0].astype(F32), piece[1].astype(F32), grad[...].astype(F32)
        sig = jax.nn.sigmoid(gate)
        through = d_hidden * sig
        d_gates.append((through * up * (1.0 + gate * (1.0 - sig))).astype(BF16))
        d_ups.append((through * gate).astype(BF16))
    contracted = (((1,), (1,)), ((), ()))
    result = lax.dot_general(
        jnp.concatenate(d_gates, axis=0), w_gate_ref[...], contracted, preferred_element_type=F32
    ) + lax.dot_general(
        jnp.concatenate(d_ups, axis=0), w_up_ref[...], contracted, preferred_element_type=F32
    )

    @pl.when(step == 0)
    def _():
        total[...] = result if first else before[...] + result

    @pl.when(step > 0)
    def _():
        total[...] += result

    @pl.when(step == pl.num_programs(0) - 1)
    def _():
        if not last:
            out_ref[...] = total[...]
        else:
            for d in range(count // k):
                at = lax.bitwise_xor(shift_ref[0], d)
                for s in range(k):
                    start = pl.multiple_of((at * k + s) * own, 16)
                    out_ref[d, s] = total[pl.ds(start, own), :].astype(BF16)


def local(
    block_out,
    stream_mid,
    gate_pre,
    up_pre,
    final_gain,
    mlp_gain,
    value_weight,
    returns,
    response_mask,
    w_gate,
    w_up,
    w_down,
):
    rows, cols = lax.axis_size("row"), lax.axis_size("col")
    row, col = lax.axis_index("row"), lax.axis_index("col")
    k = rows // cols
    own, block = block_out.shape
    width = block * cols
    tile = width // rows
    units = gate_pre.shape[1]
    lane = row % k
    shift = lax.bitwise_xor(row // k, col).astype(jnp.int32).reshape(1)

    def across(values, bit):
        return lax.ppermute(values, "row", [(r, r ^ bit) for r in range(rows)])

    def along(values, bit):
        return lax.ppermute(values, "col", [(c, c ^ bit) for c in range(cols)])

    def swap(values, s):
        pairs = [
            (r * cols + c, (k * c + ((r % k) ^ s)) * cols + r // k)
            for r in range(rows)
            for c in range(cols)
        ]
        return lax.ppermute(values, ("row", "col"), pairs)

    links = bits_of(rows)[1:]
    orders = [links, links[::-1]]

    sums, head = call(
        sums_kernel,
        (1,),
        [whole((own, block)), whole((own, block)), whole((1, block)), whole((1, block))],
        [whole((own, LANES)), whole((1, block))],
        [jax.ShapeDtypeStruct((own, LANES), F32), jax.ShapeDtypeStruct((1, block), F32)],
        cost=cost(own * block * 6, own * block * 4),
    )(block_out, stream_mid, final_gain[None, :], value_weight[None, :])

    tiles = block_out.reshape(own, k, tile)
    pieces = [
        swap(lax.dynamic_index_in_dim(tiles, lane ^ s, axis=1, keepdims=False), s) for s in range(k)
    ]
    head_tile = swap(
        lax.dynamic_index_in_dim(head.reshape(1, k, tile), lane, axis=1, keepdims=False), 0
    )
    sums_parts = [sums] + [along(sums, d) for d in range(1, cols)]
    pieces = jnp.stack(pieces)
    pieces = [pieces] + [along(pieces, d) for d in range(1, cols)]

    token = call(
        functools.partial(token_kernel, width),
        (1,),
        [whole((own, LANES))] * cols + [whole((own, 1))] * 2,
        whole((own, LANES)),
        jax.ShapeDtypeStruct((own, LANES), F32),
        cost=cost(own * LANES * 16, own * LANES * 4 * 8),
    )(*sums_parts, returns[:, None], response_mask[:, None])
    tokens = [token] + [across(token, q) for q in range(1, rows)]

    half = units // 2

    def gather(values, order):
        held = {0: values}
        for bit in order + [1]:
            held.update({q ^ bit: across(piece, bit) for q, piece in list(held.items())})
        return [held[q] for q in range(rows)]

    paired = [
        jnp.stack([gate_pre[:, h * half : (h + 1) * half], up_pre[:, h * half : (h + 1) * half]])
        for h in range(2)
    ]
    paired = [gather(paired[h], orders[h]) for h in range(2)]

    d_out, factor = call(
        functools.partial(out_kernel, width, rows, k, own),
        (1,),
        [pl.BlockSpec(memory_space=pltpu.SMEM), whole((1, tile))]
        + [whole((own, LANES))] * rows
        + [whole((k, own, tile))] * cols,
        [whole((rows, own, tile)), whole((8, LANES))],
        [jax.ShapeDtypeStruct((rows, own, tile), BF16), jax.ShapeDtypeStruct((8, LANES), F32)],
        cost=cost(rows * own * tile * 6, rows * own * tile * 4),
    )(shift, head_tile, *tokens, *pieces)

    fb = block_of(half, 512)
    blocks = half // fb
    grads = []
    for h in range(2):
        send, keep = call(
            partial_kernel,
            (blocks,),
            [
                whole((rows, own, tile)),
                pl.BlockSpec((fb, tile), lambda i, h=h: (h * blocks + i, 0)),
            ],
            [pl.BlockSpec((rows // 2, own, fb), lambda i: (0, 0, i))] * 2,
            [jax.ShapeDtypeStruct((rows // 2, own, half), BF16)] * 2,
            cost=cost(2 * rows * own * tile * half, 2 * half * tile + 2 * rows * own * half),
        )(d_out, w_down)
        remaining = [1] + orders[h]
        positions = bits_of(rows)
        for at, bit in enumerate(remaining):
            came = across(send, bit)
            positions.remove(bit)
            if not positions:
                (own_grad,) = add(keep, came, 0)
            else:
                send, keep = add(keep, came, 1 << positions.index(remaining[at + 1]))
        grads.append(gather(own_grad, orders[h]))

    d_w_down = None
    for h in range(2):
        ins = [whole((rows, own, tile))] + [pl.BlockSpec((2, own, fb), lambda i: (0, 0, i))] * rows
        args = [d_out, *paired[h]]
        aliases = {}
        if h:
            ins.append(pl.BlockSpec(memory_space=pl.ANY))
            args.append(d_w_down)
            aliases = {len(args) - 1: 0}
        d_w_down = call(
            weight_kernel,
            (blocks,),
            ins,
            pl.BlockSpec((fb, tile), lambda i, h=h: (h * blocks + i, 0)),
            jax.ShapeDtypeStruct((units, tile), F32),
            cost=cost(
                2 * rows * own * tile * half, 4 * half * tile + 4 * rows * own * half, rows * own * half
            ),
            aliases=aliases,
        )(*args)

    total = None
    for h in range(2):
        first, last = h == 0, h == 1
        weights = pl.BlockSpec((tile, fb), lambda i, h=h: (0, h * blocks + i))
        ins = (
            [pl.BlockSpec(memory_space=pltpu.SMEM), weights, weights]
            + [pl.BlockSpec((2, own, fb), lambda i: (0, 0, i))] * rows
            + [pl.BlockSpec((own, fb), lambda i: (0, i))] * rows
        )
        args = [shift, w_gate, w_up, *paired[h], *grads[h]]
        if not first:
            ins.append(whole((rows * own, tile)))
            args.append(total)
        shape = (cols, k, own, tile) if last else (rows * own, tile)
        total = call(
            functools.partial(normed_kernel, first, last, k),
            (blocks,),
            ins,
            whole(shape),
            jax.ShapeDtypeStruct(shape, BF16 if last else F32),
            scratch=[pltpu.VMEM((rows * own, tile), F32)],
            cost=cost(
                4 * rows * own * tile * half, 4 * half * tile + 6 * rows * own * half, rows * own * half
            ),
        )(*args)

    for bit in bits_of(cols):
        split = total.reshape(total.shape[0] // 2, 2, *total.shape[1:])
        total = (split[:, 0].astype(F32) + along(split[:, 1], bit).astype(F32)).astype(BF16)
    quarter = total[0]
    back = [swap(quarter[s], s).astype(F32) for s in range(k)]
    d_normed = jnp.concatenate(
        [
            functools.reduce(
                lambda other, s, j=j: jnp.where(lane ^ j == s, back[s], other), range(1, k), back[0]
            )
            for j in range(k)
        ],
        axis=1,
    )
    scaled = d_normed * mlp_gain[None, :]
    mid_root = column(token, 4)
    normalized = stream_mid.astype(F32) * mid_root
    product = jnp.sum(scaled * normalized, axis=1, keepdims=True)
    for bit in bits_of(cols):
        product = product + along(product, bit)
    own_d_out = gradient_rows(block_out.astype(F32), token, factor[0, 0], width, head)
    gradient = own_d_out.astype(F32) + mid_root * (scaled - normalized * (product / width))
    return (gradient.astype(BF16), d_w_down)


def solution(mesh):
    placed = (
        P("row", "col"),
        P("row", "col"),
        P("row", "col"),
        P("row", "col"),
        P("col"),
        P("col"),
        P("col"),
        P("row"),
        P("row"),
        P("row", "col"),
        P("row", "col"),
        P("col", "row"),
    )
    return jax.shard_map(
        local,
        mesh=mesh,
        in_specs=placed,
        out_specs=(P("row", "col"), P("col", "row")),
        check_vma=False,
    )
```

time: 364 us -> 267 us (0.73)
  blocking collectives: 104 us -> 0 us
  matrix products: 60.4 us -> 0 us
  Pallas kernels: 0 us -> 59 us
  starting transfers between devices: 0.16 us -> 58.2 us
  waiting for transfers between devices: 169 us -> 129 us
  between operations: 14.5 us -> 1.62 us
  local copies, waits for them, and re-layouts: 1.34 us -> 11.6 us
  other arithmetic: 12.4 us -> 6.25 us
    ppermute x0 -> x56, waiting for transfers between devices: none -> 129 us  [the longest x41 97.1 us: across(): return lax.ppermute(values, 'row', [(r, r ^ bit) for r in range(rows)])]
    reduce_scatter x2 -> x0, waiting for transfers between devices: 103 us -> none  [the longest x1 82.5 us: local(): lax.psum_scatter(contract(grad_rows, w_down, 1, 1), 'row', scatter_dimens...]
    all_gather x2 -> x0, waiting for transfers between devices: 64.5 us -> none  [the longest x1 64.5 us: local(): piece = lax.all_gather(stacked, 'row', axis=1, tiled=True)]
    dot_general x4 -> x0, matrix products: 60.4 us -> none  [contract(): lax.dot_general(left, right, (((left_dim,), (right_dim,)), ((), ())), pre...]
    pallas_call x0 -> x15, Pallas kernels: none -> 59 us  [the longest x2 22.4 us: local(): call(functools.partial(normed_kernel, first, last, k), (blocks,), ins, wh...]
    ppermute x0 -> x56, starting transfers between devices: none -> 58.2 us  [the longest x10 30.3 us: along(): return lax.ppermute(values, 'col', [(c, c ^ bit) for c in range(cols)])]
    all_to_all x2 -> x0, blocking collectives: 52.8 us -> none  [the longest x1 37.9 us: local(): lax.all_to_all(normed_part, 'row', split_axis=0, concat_axis=1, tiled=True)]
    psum x3 -> x0, blocking collectives: 35 us -> none  [the longest x1 13.3 us: local(): count = lax.psum(jnp.sum(live), 'row')]
  transfers between devices with their start and end apart: 4 -> 56, of which waited for: 3 -> 23; matrix products, arithmetic and copies ran while one was open for 11% -> 2% of each run, Pallas kernels for 0% -> 12%
where the time goes in v2:
time: 267 us; the launch traced here: 266 us
  waiting for transfers between devices  129 us (48%)
  Pallas kernels  59 us (22%)
  starting transfers between devices  58.2 us (22%)
  local copies, waits for them, and re-layouts  11.6 us (4%)
  other arithmetic  6.25 us (2%)
    ppermute x41, waiting for transfers between devices, across(): return lax.ppermute(values, 'row', [(r, r ^ bit) for r in range(rows)])  97.1 us
    ppermute x10, starting transfers between devices, along(): return lax.ppermute(values, 'col', [(c, c ^ bit) for c in range(cols)])  30.3 us
    pallas_call x2, Pallas kernels, local(): call(functools.partial(normed_kernel, first, last, k), (blocks,), ins, wh...  22.4 us
    ppermute x10, waiting for transfers between devices, along(): return lax.ppermute(values, 'col', [(c, c ^ bit) for c in range(cols)])  17.7 us
    pallas_call x2, Pallas kernels, local(): call(weight_kernel, (blocks,), ins, pl.BlockSpec((fb, tile), lambda i, h=...  17.6 us
    pallas_call x2, Pallas kernels, local(): call(partial_kernel, (blocks,), [whole((rows, own, tile)), pl.BlockSpec((...  15.2 us
    ppermute x5, waiting for transfers between devices, swap(): return lax.ppermute(values, ('row', 'col'), pairs)  14.6 us
    ppermute x41, starting transfers between devices, across(): return lax.ppermute(values, 'row', [(r, r ^ bit) for r in range(rows)])  14.4 us
  transfers between devices with their start and end apart: 56, of which 23 were waited for; matrix products, arithmetic and copies ran while one was open for 2% of the time, Pallas kernels for 12%

profile of v2, /device:TPU:4, one launch (start us, length us, event | category | flops | bytes accessed | tf_op | source)
XLA Modules:
  0.0 266.1 jit_solution(17530627043621071070)
XLA Ops:
  13.9 14.1 %collective-permute-start.15 = (bf16[2,48,1024]{2,1,0:T(8,128)(2,1)S(1)}, bf16[2,48,1024]{2,1,0:T(8,128)(2,1)S(1)}, u32[]{:S(2)}, u32[]{:S(2)}) collective-permute-start(bf16[2,48,1024]{2,1,0:T(8,128)(2,1)S(1)} %pad_maximum_fusion.2.refs_8_), channel_id=1, source_target_pairs={{0,3},{1,2},{2,1},{3,0},{4,7},{5,6},{6,5},{7,4},{8,11},{9,10},{10,... | collective-permute-start | bytes 589832 | tf_op jit(solution)/shard_map/ppermute | solution.py:256
  33.5 7.5 %collective-permute-done.3.head_ref = f32[1,1024]{1,0:T(1,128)S(1)} collective-permute-done((f32[1,1024]{1,0:T(1,128)S(1)}, f32[1,1024]{1,0:T(1,128)S(1)}, u32[]{:S(2)}, u32[]{:S(2)}) %collective-permute-start.3) | collective-permute-done | bytes 4128 | tf_op jit(solution)/shard_map/ppermute | solution.py:264
  41.0 4.7 %collective-permute-done.9.refs_6_ = f32[48,128]{1,0:T(8,128)S(1)} collective-permute-done((f32[48,128]{1,0:T(8,128)S(1)}, f32[48,128]{1,0:T(8,128)S(1)}, u32[]{:S(2)}, u32[]{:S(2)}) %collective-permute-start.9) | collective-permute-done | bytes 24608 | tf_op jit(solution)/shard_map/ppermute | solution.py:253
  45.8 3.8 %collective-permute-done.7.refs_4_ = f32[48,128]{1,0:T(8,128)S(1)} collective-permute-done((f32[48,128]{1,0:T(8,128)S(1)}, f32[48,128]{1,0:T(8,128)S(1)}, u32[]{:S(2)}, u32[]{:S(2)}) %collective-permute-start.7) | collective-permute-done | bytes 24608 | tf_op jit(solution)/shard_map/ppermute | solution.py:253
  49.6 3.8 %collective-permute-done.5.refs_2_ = f32[48,128]{1,0:T(8,128)S(1)} collective-permute-done((f32[48,128]{1,0:T(8,128)S(1)}, f32[48,128]{1,0:T(8,128)S(1)}, u32[]{:S(2)}, u32[]{:S(2)}) %collective-permute-start.5) | collective-permute-done | bytes 24608 | tf_op jit(solution)/shard_map/ppermute | solution.py:253
  54.1 7.5 %shard_map.138 = (bf16[4,48,3584]{2,1,0:T(8,128)(2,1)S(1)}, bf16[4,48,3584]{2,1,0:T(8,128)(2,1)S(1)}) custom-call(bf16[8,48,1024]{2,1,0:T(8,128)(2,1)S(1)} %get-tuple-element.21.d_out_ref, bf16[7168,1024]{1,0:T(8,128)(2,1)} %w_ref.3), custom_call_target="tpu_custom_call" | custom-call | flops 2818572288 | bytes 10092544 | tf_op jit(solution)/shard_map/pallas_call | solution.py:328
  61.6 7.7 %shard_map.134 = (bf16[4,48,3584]{2,1,0:T(8,128)(2,1)S(1)}, bf16[4,48,3584]{2,1,0:T(8,128)(2,1)S(1)}) custom-call(bf16[8,48,1024]{2,1,0:T(8,128)(2,1)S(1)} %get-tuple-element.21.d_out_ref, bf16[7168,1024]{1,0:T(8,128)(2,1)} %w_ref.3), custom_call_target="tpu_custom_call" | custom-call | flops 2818572288 | bytes 10092544 | tf_op jit(solution)/shard_map/pallas_call | solution.py:328
  73.3 15.2 %collective-permute-done.19.refs_4_ = bf16[2,48,3584]{2,1,0:T(8,128)(2,1)S(1)} collective-permute-done((bf16[2,48,3584]{2,1,0:T(8,128)(2,1)S(1)}, bf16[2,48,3584]{2,1,0:T(8,128)(2,1)S(1)}, u32[]{:S(2)}, u32[]{:S(2)}) %collective-permute-start.19) | collective-permute-done | bytes 688160 | tf_op jit(solution)/shard_map/ppermute | solution.py:253
  91.4 11.8 %collective-permute-done.36.refs_4_ = bf16[2,48,3584]{2,1,0:T(8,128)(2,1)S(1)} collective-permute-done((bf16[2,48,3584]{2,1,0:T(8,128)(2,1)S(1)}, bf16[2,48,3584]{2,1,0:T(8,128)(2,1)S(1)}, u32[]{:S(2)}, u32[]{:S(2)}) %collective-permute-start.36) | collective-permute-done | bytes 688160 | tf_op jit(solution)/shard_map/ppermute | solution.py:253
  103.2 3.6 %collective-permute-done.34.refs_2_ = bf16[2,48,3584]{2,1,0:T(8,128)(2,1)S(1)} collective-permute-done((bf16[2,48,3584]{2,1,0:T(8,128)(2,1)S(1)}, bf16[2,48,3584]{2,1,0:T(8,128)(2,1)S(1)}, u32[]{:S(2)}, u32[]{:S(2)}) %collective-permute-start.34) | collective-permute-done | bytes 688160 | tf_op jit(solution)/shard_map/ppermute | solution.py:253
  106.8 14.7 %collective-permute-done.41.came_ref = bf16[2,48,3584]{2,1,0:T(8,128)(2,1)S(1)} collective-permute-done((bf16[2,48,3584]{2,1,0:T(8,128)(2,1)S(1)}, bf16[2,48,3584]{2,1,0:T(8,128)(2,1)S(1)}, u32[]{:S(2)}, u32[]{:S(2)}) %collective-permute-start.41) | collective-permute-done | bytes 688160 | tf_op jit(solution)/shard_map/ppermute | solution.py:253
  124.6 9.0 %collective-permute-done.21.refs_6_ = bf16[2,48,3584]{2,1,0:T(8,128)(2,1)S(1)} collective-permute-done((bf16[2,48,3584]{2,1,0:T(8,128)(2,1)S(1)}, bf16[2,48,3584]{2,1,0:T(8,128)(2,1)S(1)}, u32[]{:S(2)}, u32[]{:S(2)}) %collective-permute-start.21) | collective-permute-done | bytes 688160 | tf_op jit(solution)/shard_map/ppermute | solution.py:253
  147.7 4.3 %collective-permute-done.44.refs_10_ = bf16[48,3584]{1,0:T(8,128)(2,1)S(1)} collective-permute-done((bf16[48,3584]{1,0:T(8,128)(2,1)S(1)}, bf16[48,3584]{1,0:T(8,128)(2,1)S(1)}, u32[]{:S(2)}, u32[]{:S(2)}) %collective-permute-start.44) | collective-permute-done | bytes 344096 | tf_op jit(solution)/shard_map/ppermute | solution.py:253
  156.8 6.9 %collective-permute-done.29.refs_12_ = bf16[48,3584]{1,0:T(8,128)(2,1)S(1)} collective-permute-done((bf16[48,3584]{1,0:T(8,128)(2,1)S(1)}, bf16[48,3584]{1,0:T(8,128)(2,1)S(1)}, u32[]{:S(2)}, u32[]{:S(2)}) %collective-permute-start.29) | collective-permute-done | bytes 344096 | tf_op jit(solution)/shard_map/ppermute | solution.py:253
  171.4 11.1 %shard_map.142.refs_16_ = f32[384,1024]{1,0:T(8,128)S(1)} custom-call(s32[1]{0:T(128)} %bitcast.5.shift_ref, bf16[1024,7168]{1,0:T(8,128)(2,1)} %w_gate_ref.3, bf16[1024,7168]{1,0:T(8,128)(2,1)} %w_up_ref.3, bf16[2,48,3584]{2,1,0:T(8,128)(2,1)S(1)} %pad_maximum_fusion.1.refs_0_, bf16[2,48,3584]{2,1,0:T(8,128)(2,1)S(1)} %collective-permute-done.33.refs_1_, ...), custom_call_target="tpu_custom_call" | custom-call | flops 5637144576 | bytes 22937600 | tf_op jit(solution)/shard_map/pallas_call | solution.py:385
  182.6 11.3 %shard_map.143 = bf16[4,2,48,1024]{3,2,1,0:T(8,128)(2,1)S(1)} custom-call(s32[1]{0:T(128)} %bitcast.5.shift_ref, bf16[1024,7168]{1,0:T(8,128)(2,1)} %w_gate_ref.3, bf16[1024,7168]{1,0:T(8,128)(2,1)} %w_up_ref.3, bf16[2,48,3584]{2,1,0:T(8,128)(2,1)S(1)} %pad_maximum_fusion.refs_0_, bf16[2,48,3584]{2,1,0:T(8,128)(2,1)S(1)} %collective-permute-done.16.refs_1_, ...), custom_call_target="tpu_custom_call" | custom-call | flops 5637144576 | bytes 22937600 | tf_op jit(solution)/shard_map/pallas_call | solution.py:385
  195.7 9.4 %collective-permute-done.50 = bf16[2,2,48,1024]{3,2,1,0:T(8,128)(2,1)S(1)} collective-permute-done((bf16[2,2,48,1024]{3,2,1,0:T(8,128)(2,1)S(1)}, bf16[2,2,48,1024]{3,2,1,0:T(8,128)(2,1)S(1)}, u32[]{:S(2)}, u32[]{:S(2)}) %collective-permute-start.50) | collective-permute-done | bytes 393248 | tf_op jit(solution)/shard_map/ppermute | solution.py:256
  206.7 4.2 %collective-permute-start.51 = (bf16[1,2,48,1024]{3,2,1,0:T(8,128)(2,1)}, bf16[1,2,48,1024]{3,2,1,0:T(8,128)(2,1)}, u32[]{:S(2)}, u32[]{:S(2)}) collective-permute-start(bf16[1,2,48,1024]{3,2,1,0:T(8,128)(2,1)} %slice_bitcast_fusion.6), channel_id=1, source_target_pairs={{0,2},{1,3},{2,0},{3,1},{4,6},{5,7},{6,4},{7,5},{8,10},{9,11},{10,... | collective-permute-start | bytes 589832 | tf_op jit(solution)/shard_map/ppermute | solution.py:256
  211.4 8.2 %collective-permute-done.51 = bf16[1,2,48,1024]{3,2,1,0:T(8,128)(2,1)} collective-permute-done((bf16[1,2,48,1024]{3,2,1,0:T(8,128)(2,1)}, bf16[1,2,48,1024]{3,2,1,0:T(8,128)(2,1)}, u32[]{:S(2)}, u32[]{:S(2)}) %collective-permute-start.51) | collective-permute-done | bytes 196640 | tf_op jit(solution)/shard_map/ppermute | solution.py:256
  220.8 5.5 %collective-permute-start.53 = (bf16[48,1024]{1,0:T(8,128)(2,1)S(1)}, bf16[48,1024]{1,0:T(8,128)(2,1)S(1)}, u32[]{:S(2)}, u32[]{:S(2)}) collective-permute-start(bf16[48,1024]{1,0:T(8,128)(2,1)S(1)} %get-tuple-element.45), channel_id=1, source_target_pairs={{0,0},{1,8},{2,16},{3,24},{4,4},{5,12},{6,20},{7,28},{8,1},{9,9},{... | collective-permute-start | bytes 294920 | tf_op jit(solution)/shard_map/ppermute | solution.py:264
  229.8 4.4 %collective-permute-done.53 = bf16[48,1024]{1,0:T(8,128)(2,1)S(1)} collective-permute-done((bf16[48,1024]{1,0:T(8,128)(2,1)S(1)}, bf16[48,1024]{1,0:T(8,128)(2,1)S(1)}, u32[]{:S(2)}, u32[]{:S(2)}) %collective-permute-start.53) | collective-permute-done | bytes 98336 | tf_op jit(solution)/shard_map/ppermute | solution.py:264
  241.9 8.8 %shard_map.144.refs_8_ = f32[7168,1024]{1,0:T(8,128)} custom-call(bf16[8,48,1024]{2,1,0:T(8,128)(2,1)S(1)} %get-tuple-element.21.d_out_ref, bf16[2,48,3584]{2,1,0:T(8,128)(2,1)S(1)} %pad_maximum_fusion.1.refs_0_, bf16[2,48,3584]{2,1,0:T(8,128)(2,1)S(1)} %copy-done.1, bf16[2,48,3584]{2,1,0:T(8,128)(2,1)S(1)} %collective-permute-done.34.refs_2_, ...), custom_call_target="tpu_custom_call" | custom-call | flops 2818572288 | bytes 20185088 | tf_op jit(solution)/shard_map/pallas_call | solution.py:359
  250.8 5.3 %collective-permute-start.55 = (f32[48,1]{1,0:T(8,128)S(1)}, f32[48,1]{1,0:T(8,128)S(1)}, u32[]{:S(2)}, u32[]{:S(2)}) collective-permute-start(f32[48,1]{1,0:T(8,128)S(1)} %add.34), channel_id=1, source_target_pairs={{0,2},{1,3},{2,0},{3,1},{4,6},{5,7},{6,4},{7,5},{8,10},{9,11},{10,... | collective-permute-start | bytes 584 | tf_op jit(solution)/shard_map/ppermute | solution.py:256
  256.1 8.8 %shard_map.145 = f32[7168,1024]{1,0:T(8,128)} custom-call(bf16[8,48,1024]{2,1,0:T(8,128)(2,1)S(1)} %get-tuple-element.21.d_out_ref, bf16[2,48,3584]{2,1,0:T(8,128)(2,1)S(1)} %pad_maximum_fusion.refs_0_, bf16[2,48,3584]{2,1,0:T(8,128)(2,1)S(1)} %copy-done.15, bf16[2,48,3584]{2,1,0:T(8,128)(2,1)S(1)} %copy-done.13, ...), custom_call_target="tpu_custom_call", output_to_operand_aliasing={{}: (9, {})} | custom-call | flops 2818572288 | bytes 20185088 | tf_op jit(solution)/shard_map/pallas_call | solution.py:359
  (222 shorter events, 73.0 us)
Async XLA Ops:
  7.9 20.1 %collective-permute-start.2 = (f32[48,128]{1,0:T(8,128)S(1)}, f32[48,128]{1,0:T(8,128)S(1)}, u32[]{:S(2)}, u32[]{:S(2)}) collective-permute-start(f32[48,128]{1,0:T(8,128)S(1)} %get-tuple-element.18.refs_0_), channel_id=1, source_target_pairs={{0,3},{1,2},{2,1},{3,0},{4,7},{5,6},{6,5},{7,4},{8,11},{9,10},{10,... | collective-permute-start | bytes 73736 | tf_op jit(solution)/shard_map/ppermute | solution.py:256
  10.7 19.3 %collective-permute-start.1 = (f32[48,128]{1,0:T(8,128)S(1)}, f32[48,128]{1,0:T(8,128)S(1)}, u32[]{:S(2)}, u32[]{:S(2)}) collective-permute-start(f32[48,128]{1,0:T(8,128)S(1)} %get-tuple-element.18.refs_0_), channel_id=1, source_target_pairs={{0,2},{1,3},{2,0},{3,1},{4,6},{5,7},{6,4},{7,5},{8,10},{9,11},{10,... | collective-permute-start | bytes 73736 | tf_op jit(solution)/shard_map/ppermute | solution.py:256
  11.0 19.0 %collective-permute-start = (f32[48,128]{1,0:T(8,128)S(1)}, f32[48,128]{1,0:T(8,128)S(1)}, u32[]{:S(2)}, u32[]{:S(2)}) collective-permute-start(f32[48,128]{1,0:T(8,128)S(1)} %get-tuple-element.18.refs_0_), channel_id=1, source_target_pairs={{0,1},{1,0},{2,3},{3,2},{4,5},{5,4},{6,7},{7,6},{8,9},{9,8},{10,11... | collective-permute-start | bytes 73736 | tf_op jit(solution)/shard_map/ppermute | solution.py:256
  13.9 39.5 %collective-permute-start.15 = (bf16[2,48,1024]{2,1,0:T(8,128)(2,1)S(1)}, bf16[2,48,1024]{2,1,0:T(8,128)(2,1)S(1)}, u32[]{:S(2)}, u32[]{:S(2)}) collective-permute-start(bf16[2,48,1024]{2,1,0:T(8,128)(2,1)S(1)} %pad_maximum_fusion.2.refs_8_), channel_id=1, source_target_pairs={{0,3},{1,2},{2,1},{3,0},{4,7},{5,6},{6,5},{7,4},{8,11},{9,10},{10,... | collective-permute-start | bytes 589832 | tf_op jit(solution)/shard_map/ppermute | solution.py:256
  28.0 25.4 %collective-permute-start.14 = (bf16[2,48,1024]{2,1,0:T(8,128)(2,1)S(1)}, bf16[2,48,1024]{2,1,0:T(8,128)(2,1)S(1)}, u32[]{:S(2)}, u32[]{:S(2)}) collective-permute-start(bf16[2,48,1024]{2,1,0:T(8,128)(2,1)S(1)} %pad_maximum_fusion.2.refs_8_), channel_id=1, source_target_pairs={{0,2},{1,3},{2,0},{3,1},{4,6},{5,7},{6,4},{7,5},{8,10},{9,11},{10,... | collective-permute-start | bytes 589832 | tf_op jit(solution)/shard_map/ppermute | solution.py:256
  28.0 25.4 %collective-permute-start.13 = (bf16[2,48,1024]{2,1,0:T(8,128)(2,1)S(1)}, bf16[2,48,1024]{2,1,0:T(8,128)(2,1)S(1)}, u32[]{:S(2)}, u32[]{:S(2)}) collective-permute-start(bf16[2,48,1024]{2,1,0:T(8,128)(2,1)S(1)} %pad_maximum_fusion.2.refs_8_), channel_id=1, source_target_pairs={{0,1},{1,0},{2,3},{3,2},{4,5},{5,4},{6,7},{7,6},{8,9},{9,8},{10,11... | collective-permute-start | bytes 589832 | tf_op jit(solution)/shard_map/ppermute | solution.py:256
  69.4 19.0 %collective-permute-start.23 = (bf16[4,48,3584]{2,1,0:T(8,128)(2,1)S(1)}, bf16[4,48,3584]{2,1,0:T(8,128)(2,1)S(1)}, u32[]{:S(2)}, u32[]{:S(2)}) collective-permute-start(bf16[4,48,3584]{2,1,0:T(8,128)(2,1)S(1)} %get-tuple-element.23), channel_id=1, source_target_pairs={{0,4},{4,0},{8,12},{12,8},{16,20},{20,16},{24,28},{28,24},{1,5},{5... | collective-permute-start | bytes 4128776 | tf_op jit(solution)/shard_map/ppermute | solution.py:253
  70.1 18.4 %collective-permute-start.19 = (bf16[2,48,3584]{2,1,0:T(8,128)(2,1)S(1)}, bf16[2,48,3584]{2,1,0:T(8,128)(2,1)S(1)}, u32[]{:S(2)}, u32[]{:S(2)}) collective-permute-start(bf16[2,48,3584]{2,1,0:T(8,128)(2,1)S(1)} %pad_maximum_fusion.refs_0_), channel_id=1, source_target_pairs={{0,16},{4,20},{8,24},{12,28},{16,0},{20,4},{24,8},{28,12},{1,17},{... | collective-permute-start | bytes 2064392 | tf_op jit(solution)/shard_map/ppermute | solution.py:253
  70.1 21.1 %collective-permute-start.17 = (bf16[2,48,3584]{2,1,0:T(8,128)(2,1)S(1)}, bf16[2,48,3584]{2,1,0:T(8,128)(2,1)S(1)}, u32[]{:S(2)}, u32[]{:S(2)}) collective-permute-start(bf16[2,48,3584]{2,1,0:T(8,128)(2,1)S(1)} %pad_maximum_fusion.refs_0_), channel_id=1, source_target_pairs={{0,8},{4,12},{8,0},{12,4},{16,24},{20,28},{24,16},{28,20},{1,9},{5... | collective-permute-start | bytes 2064392 | tf_op jit(solution)/shard_map/ppermute | solution.py:253
  70.7 20.6 %collective-permute-start.16 = (bf16[2,48,3584]{2,1,0:T(8,128)(2,1)S(1)}, bf16[2,48,3584]{2,1,0:T(8,128)(2,1)S(1)}, u32[]{:S(2)}, u32[]{:S(2)}) collective-permute-start(bf16[2,48,3584]{2,1,0:T(8,128)(2,1)S(1)} %pad_maximum_fusion.refs_0_), channel_id=1, source_target_pairs={{0,4},{4,0},{8,12},{12,8},{16,20},{20,16},{24,28},{28,24},{1,5},{5... | collective-permute-start | bytes 2064392 | tf_op jit(solution)/shard_map/ppermute | solution.py:253
  72.5 30.7 %collective-permute-start.36 = (bf16[2,48,3584]{2,1,0:T(8,128)(2,1)S(1)}, bf16[2,48,3584]{2,1,0:T(8,128)(2,1)S(1)}, u32[]{:S(2)}, u32[]{:S(2)}) collective-permute-start(bf16[2,48,3584]{2,1,0:T(8,128)(2,1)S(1)} %pad_maximum_fusion.1.refs_0_), channel_id=1, source_target_pairs={{0,16},{4,20},{8,24},{12,28},{16,0},{20,4},{24,8},{28,12},{1,17},{... | collective-permute-start | bytes 2064392 | tf_op jit(solution)/shard_map/ppermute | solution.py:253
  88.4 18.4 %collective-permute-start.34 = (bf16[2,48,3584]{2,1,0:T(8,128)(2,1)S(1)}, bf16[2,48,3584]{2,1,0:T(8,128)(2,1)S(1)}, u32[]{:S(2)}, u32[]{:S(2)}) collective-permute-start(bf16[2,48,3584]{2,1,0:T(8,128)(2,1)S(1)} %pad_maximum_fusion.1.refs_0_), channel_id=1, source_target_pairs={{0,8},{4,12},{8,0},{12,4},{16,24},{20,28},{24,16},{28,20},{1,9},{5... | collective-permute-start | bytes 2064392 | tf_op jit(solution)/shard_map/ppermute | solution.py:253
  88.4 33.1 %collective-permute-start.41 = (bf16[2,48,3584]{2,1,0:T(8,128)(2,1)S(1)}, bf16[2,48,3584]{2,1,0:T(8,128)(2,1)S(1)}, u32[]{:S(2)}, u32[]{:S(2)}) collective-permute-start(bf16[2,48,3584]{2,1,0:T(8,128)(2,1)S(1)} %get-tuple-element.31), channel_id=1, source_target_pairs={{0,8},{4,12},{8,0},{12,4},{16,24},{20,28},{24,16},{28,20},{1,9},{5... | collective-permute-start | bytes 2064392 | tf_op jit(solution)/shard_map/ppermute | solution.py:253
  91.2 30.8 %collective-permute-start.24 = (bf16[2,48,3584]{2,1,0:T(8,128)(2,1)S(1)}, bf16[2,48,3584]{2,1,0:T(8,128)(2,1)S(1)}, u32[]{:S(2)}, u32[]{:S(2)}) collective-permute-start(bf16[2,48,3584]{2,1,0:T(8,128)(2,1)S(1)} %get-tuple-element.25), channel_id=1, source_target_pairs={{0,16},{4,20},{8,24},{12,28},{16,0},{20,4},{24,8},{28,12},{1,17},{... | collective-permute-start | bytes 2064392 | tf_op jit(solution)/shard_map/ppermute | solution.py:253
  91.3 33.2 %collective-permute-start.33 = (bf16[2,48,3584]{2,1,0:T(8,128)(2,1)S(1)}, bf16[2,48,3584]{2,1,0:T(8,128)(2,1)S(1)}, u32[]{:S(2)}, u32[]{:S(2)}) collective-permute-start(bf16[2,48,3584]{2,1,0:T(8,128)(2,1)S(1)} %pad_maximum_fusion.1.refs_0_), channel_id=1, source_target_pairs={{0,4},{4,0},{8,12},{12,8},{16,20},{20,16},{24,28},{28,24},{1,5},{5... | collective-permute-start | bytes 2064392 | tf_op jit(solution)/shard_map/ppermute | solution.py:253
  103.2 30.5 %collective-permute-start.21 = (bf16[2,48,3584]{2,1,0:T(8,128)(2,1)S(1)}, bf16[2,48,3584]{2,1,0:T(8,128)(2,1)S(1)}, u32[]{:S(2)}, u32[]{:S(2)}) collective-permute-start(bf16[2,48,3584]{2,1,0:T(8,128)(2,1)S(1)} %collective-permute-done.19.refs_4_), channel_id=1, source_target_pairs={{0,8},{4,12},{8,0},{12,4},{16,24},{20,28},{24,16},{28,20},{1,9},{5... | collective-permute-start | bytes 2064392 | tf_op jit(solution)/shard_map/ppermute | solution.py:253
  106.8 26.8 %collective-permute-start.20 = (bf16[2,48,3584]{2,1,0:T(8,128)(2,1)S(1)}, bf16[2,48,3584]{2,1,0:T(8,128)(2,1)S(1)}, u32[]{:S(2)}, u32[]{:S(2)}) collective-permute-start(bf16[2,48,3584]{2,1,0:T(8,128)(2,1)S(1)} %collective-permute-done.19.refs_4_), channel_id=1, source_target_pairs={{0,4},{4,0},{8,12},{12,8},{16,20},{20,16},{24,28},{28,24},{1,5},{5... | collective-permute-start | bytes 2064392 | tf_op jit(solution)/shard_map/ppermute | solution.py:253
  121.5 15.8 %collective-permute-start.38 = (bf16[2,48,3584]{2,1,0:T(8,128)(2,1)S(1)}, bf16[2,48,3584]{2,1,0:T(8,128)(2,1)S(1)}, u32[]{:S(2)}, u32[]{:S(2)}) collective-permute-start(bf16[2,48,3584]{2,1,0:T(8,128)(2,1)S(1)} %collective-permute-done.34.refs_2_), channel_id=1, source_target_pairs={{0,16},{4,20},{8,24},{12,28},{16,0},{20,4},{24,8},{28,12},{1,17},{... | collective-permute-start | bytes 2064392 | tf_op jit(solution)/shard_map/ppermute | solution.py:253
  122.0 19.0 %collective-permute-start.42 = (bf16[1,48,3584]{2,1,0:T(8,128)(2,1)S(1)}, bf16[1,48,3584]{2,1,0:T(8,128)(2,1)S(1)}, u32[]{:S(2)}, u32[]{:S(2)}) collective-permute-start(bf16[1,48,3584]{2,1,0:T(8,128)(2,1)S(1)} %get-tuple-element.33), channel_id=1, source_target_pairs={{0,16},{4,20},{8,24},{12,28},{16,0},{20,4},{24,8},{28,12},{1,17},{... | collective-permute-start | bytes 1032200 | tf_op jit(solution)/shard_map/ppermute | solution.py:253
  124.6 21.7 %collective-permute-start.35 = (bf16[2,48,3584]{2,1,0:T(8,128)(2,1)S(1)}, bf16[2,48,3584]{2,1,0:T(8,128)(2,1)S(1)}, u32[]{:S(2)}, u32[]{:S(2)}) collective-permute-start(bf16[2,48,3584]{2,1,0:T(8,128)(2,1)S(1)} %collective-permute-done.34.refs_2_), channel_id=1, source_target_pairs={{0,4},{4,0},{8,12},{12,8},{16,20},{20,16},{24,28},{28,24},{1,5},{5... | collective-permute-start | bytes 2064392 | tf_op jit(solution)/shard_map/ppermute | solution.py:253
  146.3 17.3 %collective-permute-start.29 = (bf16[48,3584]{1,0:T(8,128)(2,1)S(1)}, bf16[48,3584]{1,0:T(8,128)(2,1)S(1)}, u32[]{:S(2)}, u32[]{:S(2)}) collective-permute-start(bf16[48,3584]{1,0:T(8,128)(2,1)S(1)} %shard_map.137.refs_8_), channel_id=1, source_target_pairs={{0,16},{4,20},{8,24},{12,28},{16,0},{20,4},{24,8},{28,12},{1,17},{... | collective-permute-start | bytes 1032200 | tf_op jit(solution)/shard_map/ppermute | solution.py:253
  152.0 15.6 %collective-permute-start.48 = (bf16[48,3584]{1,0:T(8,128)(2,1)S(1)}, bf16[48,3584]{1,0:T(8,128)(2,1)S(1)}, u32[]{:S(2)}, u32[]{:S(2)}) collective-permute-start(bf16[48,3584]{1,0:T(8,128)(2,1)S(1)} %collective-permute-done.44.refs_10_), channel_id=1, source_target_pairs={{0,16},{4,20},{8,24},{12,28},{16,0},{20,4},{24,8},{28,12},{1,17},{... | collective-permute-start | bytes 1032200 | tf_op jit(solution)/shard_map/ppermute | solution.py:253
  167.6 14.9 %collective-permute-start.22 = (bf16[2,48,3584]{2,1,0:T(8,128)(2,1)S(1)}, bf16[2,48,3584]{2,1,0:T(8,128)(2,1)S(1)}, u32[]{:S(2)}, u32[]{:S(2)}) collective-permute-start(bf16[2,48,3584]{2,1,0:T(8,128)(2,1)S(1)} %collective-permute-done.21.refs_6_), channel_id=1, source_target_pairs={{0,4},{4,0},{8,12},{12,8},{16,20},{20,16},{24,28},{28,24},{1,5},{5... | collective-permute-start | bytes 2064392 | tf_op jit(solution)/shard_map/ppermute | solution.py:253
  168.1 14.5 %collective-permute-start.26 = (bf16[48,3584]{1,0:T(8,128)(2,1)S(1)}, bf16[48,3584]{1,0:T(8,128)(2,1)S(1)}, u32[]{:S(2)}, u32[]{:S(2)}) collective-permute-start(bf16[48,3584]{1,0:T(8,128)(2,1)S(1)} %shard_map.137.refs_8_), channel_id=1, source_target_pairs={{0,4},{4,0},{8,12},{12,8},{16,20},{20,16},{24,28},{28,24},{1,5},{5... | collective-permute-start | bytes 1032200 | tf_op jit(solution)/shard_map/ppermute | solution.py:253
  (78 other events, 1324.5 us)

commit v3 on v0

v3 whole, which is shorter than its diff:
```python
import functools
import math

import jax
import jax.numpy as jnp
from jax import lax
from jax.experimental import pallas as pl
from jax.experimental.pallas import tpu as pltpu
from jax.sharding import PartitionSpec as P

epsilon = 1e-05
LANES = 128
MIB = 1024 * 1024
F32 = jnp.float32
BF16 = jnp.bfloat16


def bits_of(n):
    return [1 << i for i in range(n.bit_length() - 1)]


def block_of(extent, most):
    best = LANES
    for size in range(LANES, most + 1, LANES):
        if extent % size == 0:
            best = size
    return best


def call(kernel, grid, ins, outs, shapes, args, scratch=(), limit=40, cost=None, aliases={}, after=()):
    known, extra = len(ins), len(after)

    def body(*refs):
        kernel(*refs[:known], *refs[known + extra :])

    return pl.pallas_call(
        body,
        grid=grid,
        in_specs=list(ins) + [pl.BlockSpec(memory_space=pl.ANY)] * extra,
        out_specs=outs,
        out_shape=shapes,
        scratch_shapes=list(scratch),
        input_output_aliases=aliases,
        compiler_params=pltpu.CompilerParams(
            dimension_semantics=("arbitrary",) * len(grid), vmem_limit_bytes=limit * MIB
        ),
        cost_estimate=cost,
    )(*args, *after)


def cost(flops, moved, special=0):
    return pl.CostEstimate(flops=int(flops), bytes_accessed=int(moved), transcendentals=int(special))


def whole(shape):
    return pl.BlockSpec(shape, lambda i: (0,) * len(shape))


def column(values, position):
    return values[:, position : position + 1]


def place(columns, rows):
    lane = lax.broadcasted_iota(jnp.int32, (rows, LANES), 1)
    out = jnp.zeros((rows, LANES), F32)
    for position, values in enumerate(columns):
        out = jnp.where(lane == position, values, out)
    return out


def split_three(values):
    high = values.astype(BF16)
    rest = values - high.astype(F32)
    middle = rest.astype(BF16)
    return high, middle, (rest - middle.astype(F32)).astype(BF16)


def reverse_links(q, links):
    out = q & 1
    for i in range(links):
        out = out | (((q >> (1 + i)) & 1) << (links - i))
    return out


def other_core(j, links):
    return reverse_links(2 * j, links) | 1


def relative(place_ref, k, d):
    return lax.bitwise_xor(lax.bitwise_xor(lax.div(place_ref[0], k), place_ref[1]), d) * k


def label(place_ref, q, links):
    return jnp.where(lax.rem(place_ref[0], 2) == 1, reverse_links(q, links), q)


def tile_part(place_ref, k, s, tile):
    at = lax.bitwise_xor(lax.rem(place_ref[0], k), s)
    return pl.ds(pl.multiple_of(at * tile, LANES), tile)


def pack_kernel(place_ref, out_ref, gain_ref, weight_ref, *pieces):
    own, tile = out_ref.shape[0], pieces[0].shape[1]
    for s, piece in enumerate(pieces):
        part = tile_part(place_ref, len(pieces), s, tile)
        piece[0:own, :] = out_ref[:, part]
        if s == 0:
            head = gain_ref[:, part] * weight_ref[:, part]
            zero = jnp.zeros((1, tile), BF16)
            piece[own : own + 16, :] = jnp.concatenate([*split_three(head)] + [zero] * 13, axis=0)


def head_of(ref):
    wide = ref[...].astype(F32)
    return wide[0:1] + wide[1:2] + wide[2:3]


def turn(values):
    pad = jnp.zeros((LANES - values.shape[0], LANES), F32)
    return jnp.transpose(jnp.concatenate([values, pad], axis=0))


def sums_kernel(k, place_ref, head_ref, returns_ref, live_ref, *refs):
    pieces, sums_ref = refs[:-1], refs[-1]
    own = returns_ref.shape[1]
    head = head_of(head_ref)
    for d, piece in enumerate(pieces):
        at = relative(place_ref, k, d)
        for s in range(k):
            wide = piece[s].astype(F32)
            columns = place(
                [
                    jnp.sum(wide * wide, axis=1, keepdims=True),
                    jnp.sum(wide * head, axis=1, keepdims=True),
                ],
                own,
            )
            sums_ref[at + s] = turn(columns)[0:8]
    pad = jnp.zeros((1, LANES - own), F32)
    sublane = lax.broadcasted_iota(jnp.int32, (8, LANES), 0)
    targets = jnp.concatenate([returns_ref[...], pad], axis=1)
    live = jnp.concatenate([live_ref[...].astype(F32), pad], axis=1)
    mine = jnp.where(sublane == 2, targets, jnp.where(sublane == 3, live, 0.0))
    sums_ref[0] = sums_ref[0] + mine


def sum_rows_kernel(bit, sums_ref, came_ref, out_ref):
    for q in range(sums_ref.shape[0]):
        out_ref[q] = sums_ref[q] + came_ref[q ^ bit]


def gradient_rows(rows_of, token, head):
    root, dvalue, product = (column(token, i) for i in range(3))
    return (root * (head * dvalue - rows_of * root * product)).astype(BF16)


def out_kernel(width, k, bit, links, place_ref, head_ref, sums_ref, came_ref, *refs):
    pieces, (d_out_ref, token_ref, columns_ref) = refs[:-3], refs[-3:]
    rows, own = sums_ref.shape[0], d_out_ref.shape[1]
    head = head_of(head_ref)
    sums = [sums_ref[q] + came_ref[q ^ bit] for q in range(rows)]
    lives = functools.reduce(lambda a, b: a + b, [one[3:4] for one in sums])
    count = jnp.sum(lives, axis=1, keepdims=True)
    factor = (rows * own * math.sqrt(width)) / count
    for q, one in enumerate(sums):
        root = lax.rsqrt(one[0:1] / width + epsilon)
        value = root * one[1:2]
        dvalue = one[3:4] * (value - one[2:3]) * factor
        product = dvalue * value / width
        columns = jnp.concatenate([root, dvalue, product] + [jnp.zeros_like(root)] * 5, axis=0)
        columns_ref[q] = turn(columns)[0:own]
    token_ref[...] = columns_ref[0]
    for d, piece in enumerate(pieces):
        at = relative(place_ref, k, d)
        for s in range(k):
            d_out_ref[label(place_ref, at + s, links)] = gradient_rows(
                piece[s].astype(F32), columns_ref[at + s], head
            )


def partial_kernel(links, d_out_ref, w_ref, keep_ref, send_ref):
    count, own, tile = d_out_ref.shape
    result = lax.dot_general(
        d_out_ref[...].reshape(count * own, tile),
        w_ref[...],
        (((1,), (1,)), ((), ())),
        preferred_element_type=F32,
    ).astype(BF16)
    result = result.reshape(count, own, -1)
    for j in range(count // 2):
        keep_ref[j] = result[2 * j]
        send_ref[j] = result[other_core(j, links)]


def add_kernel(bit, keep_ref, came_ref, *outs):
    sent = kept = 0
    for q in range(keep_ref.shape[0]):
        total = (keep_ref[q].astype(F32) + came_ref[q].astype(F32)).astype(BF16)
        if len(outs) == 2 and q & bit:
            outs[1][sent] = total
            sent += 1
        else:
            outs[0][kept] = total
            kept += 1


def add(keep, came, bit, after=()):
    count, own, extent = keep.shape
    fb = block_of(extent, 2048 if count < 4 else 1024)
    block = pl.BlockSpec((count, own, fb), lambda i: (0, 0, i))
    parts = 2 if bit else 1
    out = pl.BlockSpec((count // parts, own, fb), lambda i: (0, 0, i))
    return call(
        functools.partial(add_kernel, bit),
        (extent // fb,),
        [block, block],
        [out] * parts,
        [jax.ShapeDtypeStruct((count // parts, own, extent), BF16)] * parts,
        [keep, came],
        cost=cost(count * own * extent, 6 * count * own * extent),
        after=after,
    )


def join_kernel(picks, *refs):
    for at, (i, j) in enumerate(picks):
        refs[-1][at] = refs[i][j]


def join(arrays, picks, after=()):
    own, extent = arrays[0].shape[1:]
    fb = block_of(extent, 1024)
    return call(
        functools.partial(join_kernel, picks),
        (extent // fb,),
        [pl.BlockSpec((array.shape[0], own, fb), lambda i: (0, 0, i)) for array in arrays],
        pl.BlockSpec((len(picks), own, fb), lambda i: (0, 0, i)),
        jax.ShapeDtypeStruct((len(picks), own, extent), BF16),
        arrays,
        cost=cost(0, 4 * len(picks) * own * extent),
        after=after,
    )


def every(*arrays):
    return [(i, j) for i, array in enumerate(arrays) for j in range(array.shape[0])]


def stack_kernel(*refs):
    for at, ref in enumerate(refs[:-1]):
        refs[-1][at] = ref[...]


def stack(arrays, own):
    extent = arrays[0].shape[1]
    fb = block_of(extent, 1024)
    return call(
        stack_kernel,
        (extent // fb,),
        [pl.BlockSpec((own, fb), lambda i: (0, i))] * len(arrays),
        pl.BlockSpec((len(arrays), own, fb), lambda i: (0, 0, i)),
        jax.ShapeDtypeStruct((len(arrays), own, extent), BF16),
        arrays,
        cost=cost(0, 4 * len(arrays) * own * extent),
    )


def weight_kernel(links, d_out_ref, mine_ref, other_ref, *refs):
    out_ref, done_ref = refs[-2:]
    count, own, tile = d_out_ref.shape
    hidden = [None] * count
    for j in range(count // 2):
        for ref, position in ((mine_ref, 2 * j), (other_ref, other_core(j, links))):
            gate, up = ref[2 * j].astype(F32), ref[2 * j + 1].astype(F32)
            hidden[position] = (gate * jax.nn.sigmoid(gate) * up).astype(BF16)
    out_ref[...] = lax.dot_general(
        jnp.concatenate(hidden, axis=0),
        d_out_ref[...].reshape(count * own, tile),
        (((0,), (0,)), ((), ())),
        preferred_element_type=F32,
    )
    done_ref[...] = jnp.zeros_like(done_ref)


def normed_kernel(links, first, last, k, place_ref, w_gate_ref, w_up_ref, mine_ref, other_ref, *refs):
    (mine_grad, other_grad), (out_ref, total) = refs[:2], refs[-2:]
    before = None if first else refs[2]
    count, own = 2 * mine_grad.shape[0], mine_grad.shape[1]
    step = pl.program_id(0)

    d_gates, d_ups = [None] * count, [None] * count
    for j in range(count // 2):
        for ref, grad, position in (
            (mine_ref, mine_grad, 2 * j),
            (other_ref, other_grad, other_core(j, links)),
        ):
            gate, up = ref[2 * j].astype(F32), ref[2 * j + 1].astype(F32)
            sig = jax.nn.sigmoid(gate)
            through = grad[j].astype(F32) * sig
            d_gates[position] = (through * up * (1.0 + gate * (1.0 - sig))).astype(BF16)
            d_ups[position] = (through * gate).astype(BF16)
    contracted = (((1,), (1,)), ((), ()))
    result = lax.dot_general(
        jnp.concatenate(d_gates, axis=0), w_gate_ref[...], contracted, preferred_element_type=F32
    ) + lax.dot_general(
        jnp.concatenate(d_ups, axis=0), w_up_ref[...], contracted, preferred_element_type=F32
    )

    @pl.when(step == 0)
    def _():
        total[...] = result if first else before[...] + result

    @pl.when(step > 0)
    def _():
        total[...] += result

    @pl.when(step == pl.num_programs(0) - 1)
    def _():
        if not last:
            out_ref[...] = total[...]
        else:
            for d in range(count // k):
                at = relative(place_ref, k, d)
                for s in range(k):
                    start = pl.multiple_of(label(place_ref, at + s, links) * own, 16)
                    out_ref[d * k + s] = total[pl.ds(start, own), :].astype(BF16)


def product_kernel(k, place_ref, mid_ref, gain_ref, *refs):
    backs, sums_ref = refs[:-1], refs[-1]
    own, tile = backs[0].shape
    products = squares = jnp.zeros((own, 1), F32)
    for s, back in enumerate(backs):
        part = tile_part(place_ref, k, s, tile)
        middle = mid_ref[:, part].astype(F32)
        products = products + jnp.sum(
            back[...].astype(F32) * gain_ref[:, part] * middle, axis=1, keepdims=True
        )
        squares = squares + jnp.sum(middle * middle, axis=1, keepdims=True)
    sums_ref[...] = place([products, squares], own)


def pair_kernel(first_ref, second_ref, out_ref):
    out_ref[...] = first_ref[...] + second_ref[...]


def result_kernel(width, k, place_ref, block_ref, mid_ref, norm_ref, weight_ref, gain_ref, token_ref, *refs):
    (sums_ref, came_ref), backs, out_ref = refs[:2], refs[2:-1], refs[-1]
    tile = backs[0].shape[1]
    sums = sums_ref[...] + came_ref[...]
    root = lax.rsqrt(column(sums, 1) / width + epsilon)
    product = column(sums, 0) * root / width
    for s, back in enumerate(backs):
        part = tile_part(place_ref, k, s, tile)
        own_d_out = gradient_rows(
            block_ref[:, part].astype(F32), token_ref[...], norm_ref[:, part] * weight_ref[:, part]
        )
        scaled = back[...].astype(F32) * gain_ref[:, part]
        normalized = mid_ref[:, part].astype(F32) * root
        out_ref[:, part] = (own_d_out.astype(F32) + root * (scaled - normalized * product)).astype(BF16)


def local(
    block_out,
    stream_mid,
    gate_pre,
    up_pre,
    final_gain,
    mlp_gain,
    value_weight,
    returns,
    response_mask,
    w_gate,
    w_up,
    w_down,
):
    rows, cols = lax.axis_size("row"), lax.axis_size("col")
    k = rows // cols
    own, block = block_out.shape
    width = block * cols
    tile = width // rows
    units = gate_pre.shape[1]
    where = jnp.stack([lax.axis_index("row"), lax.axis_index("col")]).astype(jnp.int32)
    smem = pl.BlockSpec(memory_space=pltpu.SMEM)
    final_gain, mlp_gain, value_weight = final_gain[None, :], mlp_gain[None, :], value_weight[None, :]

    link_bits = bits_of(rows)[1:]
    links = len(link_bits)

    def across(values, bit):
        return lax.ppermute(values, "row", [(r, r ^ bit) for r in range(rows)])

    def linked(values, i):
        pairs = [(r, r ^ link_bits[links - 1 - i if r % 2 else i]) for r in range(rows)]
        return lax.ppermute(values, "row", pairs)

    def along(values, bit):
        return lax.ppermute(values, "col", [(c, c ^ bit) for c in range(cols)])

    def swap(values, s):
        pairs = [
            (r * cols + c, (k * c + ((r % k) ^ s)) * cols + r // k)
            for r in range(rows)
            for c in range(cols)
        ]
        return lax.ppermute(values, ("row", "col"), pairs)

    paired = stack([gate_pre, up_pre], own)
    hop_a = linked(paired, 0)
    gate_b = linked(gate_pre[None], 1)

    shapes = [(own + 16 * (s == 0), tile) for s in range(k)]
    packed = call(
        pack_kernel,
        (1,),
        [smem, whole((own, block)), whole((1, block)), whole((1, block))],
        [whole(shape) for shape in shapes],
        [jax.ShapeDtypeStruct(shape, BF16) for shape in shapes],
        [where, block_out, final_gain, value_weight],
        cost=cost(own * block, own * block * 4),
    )
    swapped = [swap(packed[s], s) for s in range(k)]
    pieces = stack(swapped, own)
    pieces = [pieces] + [along(pieces, d) for d in range(1, cols)]
    head_spec = pl.BlockSpec((16, tile), lambda i: (own // 16, 0))

    more = join([paired, hop_a], [(0, 1), (1, 0), (1, 1)], after=pieces + [gate_b])
    piece_specs = [whole((k, own, tile))] * cols
    sums = call(
        functools.partial(sums_kernel, k),
        (1,),
        [smem, head_spec, whole((1, own)), whole((1, own))] + piece_specs,
        whole((rows, 8, LANES)),
        jax.ShapeDtypeStruct((rows, 8, LANES), F32),
        [where, swapped[0], returns[None, :], response_mask[None, :], *pieces],
        cost=cost(rows * own * tile * 4, rows * own * tile * 2),
        after=[more],
    )
    more_b = linked(more, 1)
    for bit in bits_of(rows)[:-1]:
        sums = call(
            functools.partial(sum_rows_kernel, bit),
            (1,),
            [whole((rows, 8, LANES))] * 2,
            whole((rows, 8, LANES)),
            jax.ShapeDtypeStruct((rows, 8, LANES), F32),
            [sums, across(sums, bit)],
            cost=cost(rows * 8 * LANES, rows * 8 * LANES * 12),
        )
    bit = bits_of(rows)[-1]
    d_out, token = call(
        functools.partial(out_kernel, width, k, bit, links),
        (1,),
        [smem, head_spec] + [whole((rows, 8, LANES))] * 2 + piece_specs,
        [whole((rows, own, tile)), whole((own, LANES))],
        [jax.ShapeDtypeStruct((rows, own, tile), BF16), jax.ShapeDtypeStruct((own, LANES), F32)],
        [where, swapped[0], sums, across(sums, bit), *pieces],
        scratch=[pltpu.VMEM((rows, own, LANES), F32)],
        cost=cost(rows * own * tile * 6, rows * own * tile * 4),
    )

    lines = units // LANES
    sizes = [lines * 5 // 14, lines * 5 // 14]
    sizes = [size * LANES for size in sizes + [lines - sum(sizes)]]
    chunks = [(sum(sizes[:i]), size) for i, size in enumerate(sizes)]
    grads, partial_sums = [], []
    for start, extent in chunks:
        fb = block_of(math.gcd(start, extent), 1024)
        keep, send = call(
            functools.partial(partial_kernel, links),
            (extent // fb,),
            [
                whole((rows, own, tile)),
                pl.BlockSpec((fb, tile), lambda i, f=start // fb: (f + i, 0)),
            ],
            [pl.BlockSpec((rows // 2, own, fb), lambda i: (0, 0, i))] * 2,
            [jax.ShapeDtypeStruct((rows // 2, own, extent), BF16)] * 2,
            [d_out, w_down],
            cost=cost(2 * rows * own * tile * extent, 2 * extent * tile + 2 * rows * own * extent),
        )
        partial_sums.append(send)
        received = across(send, 1)
        for i in range(links):
            keep, send = add(keep, received, 1)
            received = linked(send, i)
        (keep,) = add(keep, received, 0)
        for i in range(links - 1):
            came = linked(keep, i)
            keep = join([keep, came], every(keep, came))
        grads.append((keep, linked(keep, links - 1)))

    mine = join(
        [paired, hop_a, gate_b, more_b],
        every(paired, hop_a) + [(2, 0)] + [(3, j) for j in range(3)],
        after=partial_sums[1:2],
    )
    for i in range(2, links):
        came = linked(mine, i)
        mine = join([mine, came], every(mine, came))
    gathered = [mine, across(mine, 1)]

    total = None
    count = rows // 2
    for number, (start, extent) in enumerate(chunks):
        first, last = number == 0, number == len(chunks) - 1
        fb = block_of(math.gcd(start, extent), 1024)
        weights = pl.BlockSpec((tile, fb), lambda i, f=start // fb: (0, f + i))
        ins = (
            [smem, weights, weights]
            + [pl.BlockSpec((rows, own, fb), lambda i, f=start // fb: (0, 0, f + i))] * 2
            + [pl.BlockSpec((count, own, fb), lambda i: (0, 0, i))] * 2
        )
        keep, came = grads[number]
        mine = join([keep, came], every(keep, came), after=[total] if last else ())
        args = [where, w_gate, w_up, *gathered, mine, across(mine, 1)]
        if not first:
            ins.append(whole((rows * own, tile)))
            args.append(total)
        shape = (rows, own, tile) if last else (rows * own, tile)
        total = call(
            functools.partial(normed_kernel, links, first, last, k),
            (extent // fb,),
            ins,
            whole(shape),
            jax.ShapeDtypeStruct(shape, BF16 if last else F32),
            args,
            scratch=[pltpu.VMEM((rows * own, tile), F32)],
            limit=56,
            cost=cost(
                4 * rows * own * tile * extent,
                4 * extent * tile + 6 * rows * own * extent,
                rows * own * extent,
            ),
        )

    half = units // 2
    fb = block_of(half, 1024)
    blocks = half // fb
    d_w_down = None
    col_bits = bits_of(cols)
    for at, bit in enumerate(col_bits):
        n = total.shape[0] // (2 * k)
        split = total.reshape(n, 2, k, own, tile)
        keep, send = (split[:, side].reshape(n * k, own, tile) for side in range(2))
        received = along(send, bit)
        done = ()
        if at < 2:
            ins = [whole((rows, own, tile))] + [
                pl.BlockSpec((rows, own, fb), lambda i, at=at: (0, 0, at * blocks + i))
            ] * 2
            args = [d_out, *gathered]
            aliases = {}
            if at:
                ins.append(pl.BlockSpec(memory_space=pl.ANY))
                args.append(d_w_down)
                aliases = {len(args) - 1: 0}
            d_w_down, done = call(
                functools.partial(weight_kernel, links),
                (blocks,),
                ins,
                [pl.BlockSpec((fb, tile), lambda i, at=at: (at * blocks + i, 0)), whole((8, LANES))],
                [jax.ShapeDtypeStruct((units, tile), F32), jax.ShapeDtypeStruct((8, LANES), F32)],
                args,
                cost=cost(
                    2 * rows * own * tile * half,
                    4 * half * tile + 4 * rows * own * half,
                    rows * own * half,
                ),
                aliases=aliases,
                after=[total],
                limit=56,
            )
            done = (done,)
        (total,) = add(keep, received, 0, after=done)

    backs = [swap(total[s], s) for s in range(k)]
    row_spec, gain_spec = whole((own, block)), whole((1, block))
    sums_spec, back_specs = whole((own, LANES)), [whole((own, tile))] * k
    sums = call(
        functools.partial(product_kernel, k),
        (1,),
        [smem, row_spec, gain_spec] + back_specs,
        sums_spec,
        jax.ShapeDtypeStruct((own, LANES), F32),
        [where, stream_mid, mlp_gain, *backs],
        cost=cost(own * block * 5, own * block * 4),
    )
    for bit in col_bits[:-1]:
        sums = call(
            pair_kernel,
            (1,),
            [sums_spec] * 2,
            sums_spec,
            jax.ShapeDtypeStruct((own, LANES), F32),
            [sums, along(sums, bit)],
            cost=cost(own * LANES, own * LANES * 12),
        )
    gradient = call(
        functools.partial(result_kernel, width, k),
        (1,),
        [smem, row_spec, row_spec] + [gain_spec] * 3 + [sums_spec] * 3 + back_specs,
        row_spec,
        jax.ShapeDtypeStruct((own, block), BF16),
        [where, block_out, stream_mid, final_gain, value_weight, mlp_gain, token, sums]
        + [along(sums, col_bits[-1]), *backs],
        cost=cost(own * block * 14, own * block * 8),
    )
    return (gradient, d_w_down)


def solution(mesh):
    placed = (
        P("row", "col"),
        P("row", "col"),
        P("row", "col"),
        P("row", "col"),
        P("col"),
        P("col"),
        P("col"),
        P("row"),
        P("row"),
        P("row", "col"),
        P("row", "col"),
        P("col", "row"),
    )
    return jax.shard_map(
        local,
        mesh=mesh,
        in_specs=placed,
        out_specs=(P("row", "col"), P("col", "row")),
        check_vma=False,
    )
```

time: 364 us -> 254 us (0.70)
  blocking collectives: 104 us -> 0 us
  Pallas kernels: 0 us -> 83.3 us
  matrix products: 60.4 us -> 0 us
  waiting for transfers between devices: 169 us -> 110 us
  starting transfers between devices: 0.16 us -> 46.2 us
  between operations: 14.5 us -> 1.19 us
  other arithmetic: 12.4 us -> 0.07 us
  local copies, waits for them, and re-layouts: 1.34 us -> 9.37 us
    ppermute x0 -> x36, waiting for transfers between devices: none -> 110 us  [the longest x15 45.1 us: linked(): return lax.ppermute(values, 'row', pairs)]
    reduce_scatter x2 -> x0, waiting for transfers between devices: 103 us -> none  [the longest x1 82.5 us: local(): lax.psum_scatter(contract(grad_rows, w_down, 1, 1), 'row', scatter_dimens...]
    pallas_call x0 -> x37, Pallas kernels: none -> 83.3 us  [call(): pl.pallas_call(body, grid=grid, in_specs=list(ins) + [pl.BlockSpec(memory...]
    all_gather x2 -> x0, waiting for transfers between devices: 64.5 us -> none  [the longest x1 64.5 us: local(): piece = lax.all_gather(stacked, 'row', axis=1, tiled=True)]
    dot_general x4 -> x0, matrix products: 60.4 us -> none  [contract(): lax.dot_general(left, right, (((left_dim,), (right_dim,)), ((), ())), pre...]
    all_to_all x2 -> x0, blocking collectives: 52.8 us -> none  [the longest x1 37.9 us: local(): lax.all_to_all(normed_part, 'row', split_axis=0, concat_axis=1, tiled=True)]
    ppermute x0 -> x36, starting transfers between devices: none -> 46.2 us  [the longest x7 18.2 us: along(): return lax.ppermute(values, 'col', [(c, c ^ bit) for c in range(cols)])]
    psum x3 -> x0, blocking collectives: 35 us -> none  [the longest x1 13.3 us: local(): count = lax.psum(jnp.sum(live), 'row')]
  transfers between devices with their start and end apart: 4 -> 36, of which waited for: 3 -> 20; matrix products, arithmetic and copies ran while one was open for 11% -> 0% of each run, Pallas kernels for 0% -> 25%
where the time goes in v3:
time: 254 us; the launch traced here: 250 us
  waiting for transfers between devices  110 us (43%)
  Pallas kernels  83.3 us (33%)
  starting transfers between devices  46.2 us (18%)
  local copies, waits for them, and re-layouts  9.37 us (4%)
    pallas_call x37, Pallas kernels, call(): pl.pallas_call(body, grid=grid, in_specs=list(ins) + [pl.BlockSpec(memory...  83.3 us
    ppermute x15, waiting for transfers between devices, linked(): return lax.ppermute(values, 'row', pairs)  45.1 us
    ppermute x10, waiting for transfers between devices, across(): return lax.ppermute(values, 'row', [(r, r ^ bit) for r in range(rows)])  27.7 us
    ppermute x7, waiting for transfers between devices, along(): return lax.ppermute(values, 'col', [(c, c ^ bit) for c in range(cols)])  19.7 us
    ppermute x7, starting transfers between devices, along(): return lax.ppermute(values, 'col', [(c, c ^ bit) for c in range(cols)])  18.2 us
    ppermute x4, waiting for transfers between devices, swap(): return lax.ppermute(values, ('row', 'col'), pairs)  17.4 us
    ppermute x4, starting transfers between devices, swap(): return lax.ppermute(values, ('row', 'col'), pairs)  10.9 us
    ppermute x15, starting transfers between devices, linked(): return lax.ppermute(values, 'row', pairs)  9.21 us
  transfers between devices with their start and end apart: 36, of which 20 were waited for; matrix products, arithmetic and copies ran while one was open for 0% of the time, Pallas kernels for 25%

profile of v3, /device:TPU:4, one launch (start us, length us, event | category | flops | bytes accessed | tf_op | source)
XLA Modules:
  0.0 250.0 jit_solution(12068965301435580433)
XLA Ops:
  1.7 3.8 %shard_map.133.refs_0_ = bf16[2,48,7168]{2,1,0:T(8,128)(2,1)S(1)} custom-call(bf16[48,7168]{1,0:T(8,128)(2,1)} %refs_0_.1, bf16[48,7168]{1,0:T(8,128)(2,1)S(1)} %copy-done.12), custom_call_target="tpu_custom_call" | custom-call | bytes 2752512 | tf_op jit(solution)/shard_map/pallas_call | solution.py:36
  10.6 5.5 %collective-permute-start = (bf16[64,1024]{1,0:T(8,128)(2,1)S(1)}, bf16[64,1024]{1,0:T(8,128)(2,1)S(1)}, u32[]{:S(2)}, u32[]{:S(2)}) collective-permute-start(bf16[64,1024]{1,0:T(8,128)(2,1)S(1)} %get-tuple-element.28), channel_id=1, source_target_pairs={{0,0},{1,8},{2,16},{3,24},{4,4},{5,12},{6,20},{7,28},{8,1},{9,9},{... | collective-permute-start | bytes 393224 | tf_op jit(solution)/shard_map/ppermute | solution.py:406
  16.1 9.3 %collective-permute-done.1.refs_1_ = bf16[48,1024]{1,0:T(8,128)(2,1)S(1)} collective-permute-done((bf16[48,1024]{1,0:T(8,128)(2,1)S(1)}, bf16[48,1024]{1,0:T(8,128)(2,1)S(1)}, u32[]{:S(2)}, u32[]{:S(2)}) %collective-permute-start.1) | collective-permute-done | bytes 98336 | tf_op jit(solution)/shard_map/ppermute | solution.py:406
  25.4 11.5 %collective-permute-start.4 = (bf16[2,48,1024]{2,1,0:T(8,128)(2,1)S(1)}, bf16[2,48,1024]{2,1,0:T(8,128)(2,1)S(1)}, u32[]{:S(2)}, u32[]{:S(2)}) collective-permute-start(bf16[2,48,1024]{2,1,0:T(8,128)(2,1)S(1)} %shard_map.132.refs_2_.refs_4_), channel_id=1, source_target_pairs={{0,3},{1,2},{2,1},{3,0},{4,7},{5,6},{6,5},{7,4},{8,11},{9,10},{10,... | collective-permute-start | bytes 589832 | tf_op jit(solution)/shard_map/ppermute | solution.py:398
  37.6 5.1 %collective-permute-done.4.refs_5_.refs_7_ = bf16[2,48,1024]{2,1,0:T(8,128)(2,1)S(1)} collective-permute-done((bf16[2,48,1024]{2,1,0:T(8,128)(2,1)S(1)}, bf16[2,48,1024]{2,1,0:T(8,128)(2,1)S(1)}, u32[]{:S(2)}, u32[]{:S(2)}) %collective-permute-start.4) | collective-permute-done | bytes 196640 | tf_op jit(solution)/shard_map/ppermute | solution.py:398
  42.7 8.5 %collective-permute-done.3.refs_4_.refs_6_ = bf16[2,48,1024]{2,1,0:T(8,128)(2,1)S(1)} collective-permute-done((bf16[2,48,1024]{2,1,0:T(8,128)(2,1)S(1)}, bf16[2,48,1024]{2,1,0:T(8,128)(2,1)S(1)}, u32[]{:S(2)}, u32[]{:S(2)}) %collective-permute-start.3) | collective-permute-done | bytes 196640 | tf_op jit(solution)/shard_map/ppermute | solution.py:398
  60.4 17.5 %collective-permute-done.9.refs_3_ = f32[8,8,128]{2,1,0:T(8,128)S(1)} collective-permute-done((f32[8,8,128]{2,1,0:T(8,128)S(1)}, f32[8,8,128]{2,1,0:T(8,128)S(1)}, u32[]{:S(2)}, u32[]{:S(2)}) %collective-permute-start.9) | collective-permute-done | bytes 32800 | tf_op jit(solution)/shard_map/ppermute | solution.py:391
  79.2 5.6 %shard_map.139 = (bf16[4,48,2560]{2,1,0:T(8,128)(2,1)S(1)}, bf16[4,48,2560]{2,1,0:T(8,128)(2,1)S(1)}) custom-call(bf16[8,48,1024]{2,1,0:T(8,128)(2,1)S(1)} %get-tuple-element.31.refs_0_, bf16[7168,1024]{1,0:T(8,128)(2,1)} %refs_1_.14), custom_call_target="tpu_custom_call" | custom-call | flops 2013265920 | bytes 7208960 | tf_op jit(solution)/shard_map/pallas_call | solution.py:36
  84.8 4.2 %shard_map.140.refs_3_.refs_1_ = bf16[8,48,7168]{2,1,0:T(8,128)(2,1)S(1)} custom-call(bf16[2,48,7168]{2,1,0:T(8,128)(2,1)S(1)} %shard_map.133.refs_0_, bf16[2,48,7168]{2,1,0:T(8,128)(2,1)S(1)} %copy-done.4, bf16[1,48,7168]{2,1,0:T(8,128)(2,1)} %collective-permute-done.6.refs_6_.refs_2_, bf16[3,48,7168]{2,1,0:T(8,128)(2,1)S(1)} %collective-permute-done.10.refs_3_, ...), custom_call_target="tpu_custom_call" | custom-call | bytes 11010048 | tf_op jit(solution)/shard_map/pallas_call | solution.py:36
  91.4 5.3 %shard_map.151 = (bf16[4,48,2560]{2,1,0:T(8,128)(2,1)S(1)}, bf16[4,48,2560]{2,1,0:T(8,128)(2,1)S(1)}) custom-call(bf16[8,48,1024]{2,1,0:T(8,128)(2,1)S(1)} %get-tuple-element.31.refs_0_, bf16[7168,1024]{1,0:T(8,128)(2,1)} %refs_1_.14), custom_call_target="tpu_custom_call" | custom-call | flops 2013265920 | bytes 7208960 | tf_op jit(solution)/shard_map/pallas_call | solution.py:36
  104.8 6.2 %collective-permute-done.24.refs_1_ = bf16[2,48,2560]{2,1,0:T(8,128)(2,1)S(1)} collective-permute-done((bf16[2,48,2560]{2,1,0:T(8,128)(2,1)S(1)}, bf16[2,48,2560]{2,1,0:T(8,128)(2,1)S(1)}, u32[]{:S(2)}, u32[]{:S(2)}) %collective-permute-start.24) | collective-permute-done | bytes 491552 | tf_op jit(solution)/shard_map/ppermute | solution.py:395
  111.6 7.3 %collective-permute-done.18.refs_1_ = bf16[2,48,2560]{2,1,0:T(8,128)(2,1)S(1)} collective-permute-done((bf16[2,48,2560]{2,1,0:T(8,128)(2,1)S(1)}, bf16[2,48,2560]{2,1,0:T(8,128)(2,1)S(1)}, u32[]{:S(2)}, u32[]{:S(2)}) %collective-permute-start.18) | collective-permute-done | bytes 491552 | tf_op jit(solution)/shard_map/ppermute | solution.py:395
  120.8 3.7 %shard_map.141 = (bf16[4,48,2048]{2,1,0:T(8,128)(2,1)S(1)}, bf16[4,48,2048]{2,1,0:T(8,128)(2,1)S(1)}) custom-call(bf16[8,48,1024]{2,1,0:T(8,128)(2,1)S(1)} %get-tuple-element.31.refs_0_, bf16[7168,1024]{1,0:T(8,128)(2,1)} %refs_1_.14), custom_call_target="tpu_custom_call" | custom-call | flops 1610612736 | bytes 5767168 | tf_op jit(solution)/shard_map/pallas_call | solution.py:36
  128.3 8.5 %collective-permute-done.20.refs_1_ = bf16[1,48,2560]{2,1,0:T(8,128)(2,1)S(1)} collective-permute-done((bf16[1,48,2560]{2,1,0:T(8,128)(2,1)S(1)}, bf16[1,48,2560]{2,1,0:T(8,128)(2,1)S(1)}, u32[]{:S(2)}, u32[]{:S(2)}) %collective-permute-start.20) | collective-permute-done | bytes 245792 | tf_op jit(solution)/shard_map/ppermute | solution.py:395
  139.7 10.5 %collective-permute-done.21.refs_1_ = bf16[2,48,2560]{2,1,0:T(8,128)(2,1)S(1)} collective-permute-done((bf16[2,48,2560]{2,1,0:T(8,128)(2,1)S(1)}, bf16[2,48,2560]{2,1,0:T(8,128)(2,1)S(1)}, u32[]{:S(2)}, u32[]{:S(2)}) %collective-permute-start.21) | collective-permute-done | bytes 491552 | tf_op jit(solution)/shard_map/ppermute | solution.py:395
  150.8 5.7 %collective-permute-done.14.refs_1_ = bf16[1,48,2048]{2,1,0:T(8,128)(2,1)S(1)} collective-permute-done((bf16[1,48,2048]{2,1,0:T(8,128)(2,1)S(1)}, bf16[1,48,2048]{2,1,0:T(8,128)(2,1)S(1)}, u32[]{:S(2)}, u32[]{:S(2)}) %collective-permute-start.14) | collective-permute-done | bytes 196640 | tf_op jit(solution)/shard_map/ppermute | solution.py:395
  156.6 5.7 %collective-permute-done.15.refs_1_ = bf16[1,48,2048]{2,1,0:T(8,128)(2,1)S(1)} collective-permute-done((bf16[1,48,2048]{2,1,0:T(8,128)(2,1)S(1)}, bf16[1,48,2048]{2,1,0:T(8,128)(2,1)S(1)}, u32[]{:S(2)}, u32[]{:S(2)}) %collective-permute-start.15) | collective-permute-done | bytes 196640 | tf_op jit(solution)/shard_map/ppermute | solution.py:395
  163.4 10.3 %shard_map.157.refs_7_ = f32[384,1024]{1,0:T(8,128)} custom-call(s32[2]{0:T(128)} %copy-done.13, bf16[1024,7168]{1,0:T(8,128)(2,1)} %refs_1_.17, bf16[1024,7168]{1,0:T(8,128)(2,1)} %refs_2_.6, bf16[8,48,7168]{2,1,0:T(8,128)(2,1)} %copy-done, bf16[8,48,7168]{2,1,0:T(8,128)(2,1)} %collective-permute-done.11.refs_4_.refs_2_, bf16[4,48,2560]{2,1,0:T(8,128)(2,1)} %copy-done.5, ...), custom_call_target="tpu_custom_call" | custom-call | flops 4026531840 | bytes 16384000 | tf_op jit(solution)/shard_map/pallas_call | solution.py:36
  173.8 11.1 %shard_map.158.refs_2_.refs_7_ = f32[384,1024]{1,0:T(8,128)} custom-call(s32[2]{0:T(128)} %copy-done.13, bf16[1024,7168]{1,0:T(8,128)(2,1)} %refs_1_.17, bf16[1024,7168]{1,0:T(8,128)(2,1)} %refs_2_.6, bf16[8,48,7168]{2,1,0:T(8,128)(2,1)} %copy-done, bf16[8,48,7168]{2,1,0:T(8,128)(2,1)} %collective-permute-done.11.refs_4_.refs_2_, ...), custom_call_target="tpu_custom_call" | custom-call | flops 4026531840 | bytes 16384000 | tf_op jit(solution)/shard_map/pallas_call | solution.py:36
  189.8 9.2 %shard_map.160.refs_3_ = bf16[8,48,1024]{2,1,0:T(8,128)(2,1)} custom-call(s32[2]{0:T(128)} %copy-done.13, bf16[1024,7168]{1,0:T(8,128)(2,1)} %refs_1_.17, bf16[1024,7168]{1,0:T(8,128)(2,1)} %refs_2_.6, bf16[8,48,7168]{2,1,0:T(8,128)(2,1)} %copy-done, bf16[8,48,7168]{2,1,0:T(8,128)(2,1)} %collective-permute-done.11.refs_4_.refs_2_, ...), custom_call_target="tpu_custom_call" | custom-call | flops 3221225472 | bytes 13107200 | tf_op jit(solution)/shard_map/pallas_call | solution.py:36
  202.2 10.0 %shard_map.161 = (f32[7168,1024]{1,0:T(8,128)}, f32[8,128]{1,0:T(8,128)}) custom-call(bf16[8,48,1024]{2,1,0:T(8,128)(2,1)} %copy-done.1, bf16[8,48,7168]{2,1,0:T(8,128)(2,1)} %copy-done, bf16[8,48,7168]{2,1,0:T(8,128)(2,1)} %collective-permute-done.11.refs_4_.refs_2_, bf16[8,48,1024]{2,1,0:T(8,128)(2,1)} %shard_map.160.refs_3_), custom_call_target="tpu_custom_call" | custom-call | flops 2818572288 | bytes 20185088 | tf_op jit(solution)/shard_map/pallas_call | solution.py:36
  214.7 10.2 %shard_map.163 = (f32[7168,1024]{1,0:T(8,128)}, f32[8,128]{1,0:T(8,128)}) custom-call(bf16[8,48,1024]{2,1,0:T(8,128)(2,1)} %copy-done.1, bf16[8,48,7168]{2,1,0:T(8,128)(2,1)} %copy-done, bf16[8,48,7168]{2,1,0:T(8,128)(2,1)} %collective-permute-done.11.refs_4_.refs_2_, f32[7168,1024]{1,0:T(8,128)} %get-tuple-element.51.refs_3_, ...), custom_call_target="tpu_custom_call", output_to_operand_aliasing={{0}: (3, {})} | custom-call | flops 2818572288 | bytes 20185088 | tf_op jit(solution)/shard_map/pallas_call | solution.py:36
  231.1 3.6 %collective-permute-done.33.refs_4_.refs_10_ = bf16[48,1024]{1,0:T(8,128)(2,1)S(1)} collective-permute-done((bf16[48,1024]{1,0:T(8,128)(2,1)S(1)}, bf16[48,1024]{1,0:T(8,128)(2,1)S(1)}, u32[]{:S(2)}, u32[]{:S(2)}) %collective-permute-start.33) | collective-permute-done | bytes 98336 | tf_op jit(solution)/shard_map/ppermute | solution.py:406
  234.6 4.5 %collective-permute-done.32.refs_3_.refs_9_ = bf16[48,1024]{1,0:T(8,128)(2,1)S(1)} collective-permute-done((bf16[48,1024]{1,0:T(8,128)(2,1)S(1)}, bf16[48,1024]{1,0:T(8,128)(2,1)S(1)}, u32[]{:S(2)}, u32[]{:S(2)}) %collective-permute-start.32) | collective-permute-done | bytes 98336 | tf_op jit(solution)/shard_map/ppermute | solution.py:406
  (141 shorter events, 66.2 us)
Async XLA Ops:
  5.5 45.7 %collective-permute-start.5 = (bf16[2,48,7168]{2,1,0:T(8,128)(2,1)S(1)}, bf16[2,48,7168]{2,1,0:T(8,128)(2,1)S(1)}, u32[]{:S(2)}, u32[]{:S(2)}) collective-permute-start(bf16[2,48,7168]{2,1,0:T(8,128)(2,1)S(1)} %shard_map.133.refs_0_), channel_id=1, source_target_pairs={{0,8},{4,20},{8,0},{12,28},{16,24},{20,4},{24,16},{28,12},{1,9},{5... | collective-permute-start | bytes 4128776 | tf_op jit(solution)/shard_map/ppermute | solution.py:395
  7.1 44.1 %collective-permute-start.6 = (bf16[1,48,7168]{2,1,0:T(8,128)(2,1)}, bf16[1,48,7168]{2,1,0:T(8,128)(2,1)}, u32[]{:S(2)}, u32[]{:S(2)}) collective-permute-start(bf16[1,48,7168]{2,1,0:T(8,128)(2,1)} %bitcast.7), channel_id=1, source_target_pairs={{0,16},{4,12},{8,24},{12,4},{16,0},{20,28},{24,8},{28,20},{1,17},{... | collective-permute-start | bytes 2064392 | tf_op jit(solution)/shard_map/ppermute | solution.py:395
  10.6 14.8 %collective-permute-start = (bf16[64,1024]{1,0:T(8,128)(2,1)S(1)}, bf16[64,1024]{1,0:T(8,128)(2,1)S(1)}, u32[]{:S(2)}, u32[]{:S(2)}) collective-permute-start(bf16[64,1024]{1,0:T(8,128)(2,1)S(1)} %get-tuple-element.28), channel_id=1, source_target_pairs={{0,0},{1,8},{2,16},{3,24},{4,4},{5,12},{6,20},{7,28},{8,1},{9,9},{... | collective-permute-start | bytes 393224 | tf_op jit(solution)/shard_map/ppermute | solution.py:406
  16.0 9.3 %collective-permute-start.1 = (bf16[48,1024]{1,0:T(8,128)(2,1)S(1)}, bf16[48,1024]{1,0:T(8,128)(2,1)S(1)}, u32[]{:S(2)}, u32[]{:S(2)}) collective-permute-start(bf16[48,1024]{1,0:T(8,128)(2,1)S(1)} %get-tuple-element.29), channel_id=1, source_target_pairs={{0,4},{1,12},{2,20},{3,28},{4,0},{5,8},{6,16},{7,24},{8,5},{9,13},... | collective-permute-start | bytes 294920 | tf_op jit(solution)/shard_map/ppermute | solution.py:406
  25.4 17.3 %collective-permute-start.4 = (bf16[2,48,1024]{2,1,0:T(8,128)(2,1)S(1)}, bf16[2,48,1024]{2,1,0:T(8,128)(2,1)S(1)}, u32[]{:S(2)}, u32[]{:S(2)}) collective-permute-start(bf16[2,48,1024]{2,1,0:T(8,128)(2,1)S(1)} %shard_map.132.refs_2_.refs_4_), channel_id=1, source_target_pairs={{0,3},{1,2},{2,1},{3,0},{4,7},{5,6},{6,5},{7,4},{8,11},{9,10},{10,... | collective-permute-start | bytes 589832 | tf_op jit(solution)/shard_map/ppermute | solution.py:398
  36.9 14.2 %collective-permute-start.3 = (bf16[2,48,1024]{2,1,0:T(8,128)(2,1)S(1)}, bf16[2,48,1024]{2,1,0:T(8,128)(2,1)S(1)}, u32[]{:S(2)}, u32[]{:S(2)}) collective-permute-start(bf16[2,48,1024]{2,1,0:T(8,128)(2,1)S(1)} %shard_map.132.refs_2_.refs_4_), channel_id=1, source_target_pairs={{0,2},{1,3},{2,0},{3,1},{4,6},{5,7},{6,4},{7,5},{8,10},{9,11},{10,... | collective-permute-start | bytes 589832 | tf_op jit(solution)/shard_map/ppermute | solution.py:398
  36.9 14.2 %collective-permute-start.2 = (bf16[2,48,1024]{2,1,0:T(8,128)(2,1)S(1)}, bf16[2,48,1024]{2,1,0:T(8,128)(2,1)S(1)}, u32[]{:S(2)}, u32[]{:S(2)}) collective-permute-start(bf16[2,48,1024]{2,1,0:T(8,128)(2,1)S(1)} %shard_map.132.refs_2_.refs_4_), channel_id=1, source_target_pairs={{0,1},{1,0},{2,3},{3,2},{4,5},{5,4},{6,7},{7,6},{8,9},{9,8},{10,11... | collective-permute-start | bytes 589832 | tf_op jit(solution)/shard_map/ppermute | solution.py:398
  51.8 33.0 %collective-permute-start.10 = (bf16[3,48,7168]{2,1,0:T(8,128)(2,1)S(1)}, bf16[3,48,7168]{2,1,0:T(8,128)(2,1)S(1)}, u32[]{:S(2)}, u32[]{:S(2)}) collective-permute-start(bf16[3,48,7168]{2,1,0:T(8,128)(2,1)S(1)} %shard_map.134.refs_8_), channel_id=1, source_target_pairs={{0,16},{4,12},{8,24},{12,4},{16,0},{20,28},{24,8},{28,20},{1,17},{... | collective-permute-start | bytes 6193160 | tf_op jit(solution)/shard_map/ppermute | solution.py:395
  58.4 19.5 %collective-permute-start.9 = (f32[8,8,128]{2,1,0:T(8,128)S(1)}, f32[8,8,128]{2,1,0:T(8,128)S(1)}, u32[]{:S(2)}, u32[]{:S(2)}) collective-permute-start(f32[8,8,128]{2,1,0:T(8,128)S(1)} %shard_map.137.refs_2_), channel_id=1, source_target_pairs={{0,16},{4,20},{8,24},{12,28},{16,0},{20,4},{24,8},{28,12},{1,17},{... | collective-permute-start | bytes 98312 | tf_op jit(solution)/shard_map/ppermute | solution.py:391
  89.0 74.4 %collective-permute-start.11 = (bf16[8,48,7168]{2,1,0:T(8,128)(2,1)S(1)}, bf16[8,48,7168]{2,1,0:T(8,128)(2,1)}, u32[]{:S(2)}, u32[]{:S(2)}) collective-permute-start(bf16[8,48,7168]{2,1,0:T(8,128)(2,1)S(1)} %shard_map.140.refs_3_.refs_1_), channel_id=1, source_target_pairs={{0,4},{4,0},{8,12},{12,8},{16,20},{20,16},{24,28},{28,24},{1,5},{5... | collective-permute-start | bytes 16515080 | tf_op jit(solution)/shard_map/ppermute | solution.py:391
  102.1 8.9 %collective-permute-start.24 = (bf16[2,48,2560]{2,1,0:T(8,128)(2,1)S(1)}, bf16[2,48,2560]{2,1,0:T(8,128)(2,1)S(1)}, u32[]{:S(2)}, u32[]{:S(2)}) collective-permute-start(bf16[2,48,2560]{2,1,0:T(8,128)(2,1)S(1)} %get-tuple-element.47), channel_id=1, source_target_pairs={{0,8},{4,20},{8,0},{12,28},{16,24},{20,4},{24,16},{28,12},{1,9},{5... | collective-permute-start | bytes 1474568 | tf_op jit(solution)/shard_map/ppermute | solution.py:395
  103.5 15.4 %collective-permute-start.18 = (bf16[2,48,2560]{2,1,0:T(8,128)(2,1)S(1)}, bf16[2,48,2560]{2,1,0:T(8,128)(2,1)S(1)}, u32[]{:S(2)}, u32[]{:S(2)}) collective-permute-start(bf16[2,48,2560]{2,1,0:T(8,128)(2,1)S(1)} %get-tuple-element.41), channel_id=1, source_target_pairs={{0,8},{4,20},{8,0},{12,28},{16,24},{20,4},{24,16},{28,12},{1,9},{5... | collective-permute-start | bytes 1474568 | tf_op jit(solution)/shard_map/ppermute | solution.py:395
  119.2 8.8 %collective-permute-start.19 = (bf16[1,48,2560]{2,1,0:T(8,128)(2,1)S(1)}, bf16[1,48,2560]{2,1,0:T(8,128)(2,1)S(1)}, u32[]{:S(2)}, u32[]{:S(2)}) collective-permute-start(bf16[1,48,2560]{2,1,0:T(8,128)(2,1)S(1)} %get-tuple-element.43), channel_id=1, source_target_pairs={{0,16},{4,12},{8,24},{12,4},{16,0},{20,28},{24,8},{28,20},{1,17},{... | collective-permute-start | bytes 737288 | tf_op jit(solution)/shard_map/ppermute | solution.py:395
  124.5 13.3 %collective-permute-start.12 = (bf16[4,48,2048]{2,1,0:T(8,128)(2,1)S(1)}, bf16[4,48,2048]{2,1,0:T(8,128)(2,1)S(1)}, u32[]{:S(2)}, u32[]{:S(2)}) collective-permute-start(bf16[4,48,2048]{2,1,0:T(8,128)(2,1)S(1)} %get-tuple-element.34), channel_id=1, source_target_pairs={{0,4},{4,0},{8,12},{12,8},{16,20},{20,16},{24,28},{28,24},{1,5},{5... | collective-permute-start | bytes 2359304 | tf_op jit(solution)/shard_map/ppermute | solution.py:391
  126.2 11.2 %collective-permute-start.27 = (bf16[2,48,2560]{2,1,0:T(8,128)(2,1)S(1)}, bf16[2,48,2560]{2,1,0:T(8,128)(2,1)S(1)}, u32[]{:S(2)}, u32[]{:S(2)}) collective-permute-start(bf16[2,48,2560]{2,1,0:T(8,128)(2,1)S(1)} %shard_map.155.refs_0_), channel_id=1, source_target_pairs={{0,16},{4,12},{8,24},{12,4},{16,0},{20,28},{24,8},{28,20},{1,17},{... | collective-permute-start | bytes 1474568 | tf_op jit(solution)/shard_map/ppermute | solution.py:395
  137.0 13.1 %collective-permute-start.21 = (bf16[2,48,2560]{2,1,0:T(8,128)(2,1)S(1)}, bf16[2,48,2560]{2,1,0:T(8,128)(2,1)S(1)}, u32[]{:S(2)}, u32[]{:S(2)}) collective-permute-start(bf16[2,48,2560]{2,1,0:T(8,128)(2,1)S(1)} %shard_map.149.refs_0_), channel_id=1, source_target_pairs={{0,16},{4,12},{8,24},{12,4},{16,0},{20,28},{24,8},{28,20},{1,17},{... | collective-permute-start | bytes 1474568 | tf_op jit(solution)/shard_map/ppermute | solution.py:395
  137.8 24.7 %collective-permute-start.28 = (bf16[4,48,2560]{2,1,0:T(8,128)(2,1)S(1)}, bf16[4,48,2560]{2,1,0:T(8,128)(2,1)S(1)}, u32[]{:S(2)}, u32[]{:S(2)}) collective-permute-start(bf16[4,48,2560]{2,1,0:T(8,128)(2,1)S(1)} %shard_map.156.refs_5_), channel_id=1, source_target_pairs={{0,4},{4,0},{8,12},{12,8},{16,20},{20,16},{24,28},{28,24},{1,5},{5... | collective-permute-start | bytes 2949128 | tf_op jit(solution)/shard_map/ppermute | solution.py:391
  138.3 12.3 %collective-permute-start.13 = (bf16[2,48,2048]{2,1,0:T(8,128)(2,1)S(1)}, bf16[2,48,2048]{2,1,0:T(8,128)(2,1)S(1)}, u32[]{:S(2)}, u32[]{:S(2)}) collective-permute-start(bf16[2,48,2048]{2,1,0:T(8,128)(2,1)S(1)} %get-tuple-element.36), channel_id=1, source_target_pairs={{0,8},{4,20},{8,0},{12,28},{16,24},{20,4},{24,16},{28,12},{1,9},{5... | collective-permute-start | bytes 1179656 | tf_op jit(solution)/shard_map/ppermute | solution.py:395
  150.5 23.3 %collective-permute-start.22 = (bf16[4,48,2560]{2,1,0:T(8,128)(2,1)S(1)}, bf16[4,48,2560]{2,1,0:T(8,128)(2,1)}, u32[]{:S(2)}, u32[]{:S(2)}) collective-permute-start(bf16[4,48,2560]{2,1,0:T(8,128)(2,1)S(1)} %shard_map.150.refs_5_), channel_id=1, source_target_pairs={{0,4},{4,0},{8,12},{12,8},{16,20},{20,16},{24,28},{28,24},{1,5},{5... | collective-permute-start | bytes 2949128 | tf_op jit(solution)/shard_map/ppermute | solution.py:391
  162.4 22.5 %collective-permute-start.16 = (bf16[2,48,2048]{2,1,0:T(8,128)(2,1)S(1)}, bf16[2,48,2048]{2,1,0:T(8,128)(2,1)S(1)}, u32[]{:S(2)}, u32[]{:S(2)}) collective-permute-start(bf16[2,48,2048]{2,1,0:T(8,128)(2,1)S(1)} %shard_map.145.refs_0_), channel_id=1, source_target_pairs={{0,16},{4,12},{8,24},{12,4},{16,0},{20,28},{24,8},{28,20},{1,17},{... | collective-permute-start | bytes 1179656 | tf_op jit(solution)/shard_map/ppermute | solution.py:395
  200.2 12.0 %collective-permute-start.30 = (bf16[4,48,1024]{2,1,0:T(8,128)(2,1)S(1)}, bf16[4,48,1024]{2,1,0:T(8,128)(2,1)S(1)}, u32[]{:S(2)}, u32[]{:S(2)}) collective-permute-start(bf16[4,48,1024]{2,1,0:T(8,128)(2,1)S(1)} %bitcast.35), channel_id=1, source_target_pairs={{0,1},{1,0},{2,3},{3,2},{4,5},{5,4},{6,7},{7,6},{8,9},{9,8},{10,11... | collective-permute-start | bytes 1179656 | tf_op jit(solution)/shard_map/ppermute | solution.py:398
  213.1 11.8 %collective-permute-start.31 = (bf16[2,48,1024]{2,1,0:T(8,128)(2,1)S(1)}, bf16[2,48,1024]{2,1,0:T(8,128)(2,1)S(1)}, u32[]{:S(2)}, u32[]{:S(2)}) collective-permute-start(bf16[2,48,1024]{2,1,0:T(8,128)(2,1)S(1)} %get-tuple-element.56), channel_id=1, source_target_pairs={{0,2},{1,3},{2,0},{3,1},{4,6},{5,7},{6,4},{7,5},{8,10},{9,11},{10,... | collective-permute-start | bytes 589832 | tf_op jit(solution)/shard_map/ppermute | solution.py:398
  225.6 9.0 %collective-permute-start.33 = (bf16[48,1024]{1,0:T(8,128)(2,1)S(1)}, bf16[48,1024]{1,0:T(8,128)(2,1)S(1)}, u32[]{:S(2)}, u32[]{:S(2)}) collective-permute-start(bf16[48,1024]{1,0:T(8,128)(2,1)S(1)} %get-tuple-element.58), channel_id=1, source_target_pairs={{0,4},{1,12},{2,20},{3,28},{4,0},{5,8},{6,16},{7,24},{8,5},{9,13},... | collective-permute-start | bytes 294920 | tf_op jit(solution)/shard_map/ppermute | solution.py:406
  227.7 11.4 %collective-permute-start.32 = (bf16[48,1024]{1,0:T(8,128)(2,1)S(1)}, bf16[48,1024]{1,0:T(8,128)(2,1)S(1)}, u32[]{:S(2)}, u32[]{:S(2)}) collective-permute-start(bf16[48,1024]{1,0:T(8,128)(2,1)S(1)} %get-tuple-element.59), channel_id=1, source_target_pairs={{0,0},{1,8},{2,16},{3,24},{4,4},{5,12},{6,20},{7,28},{8,1},{9,9},{... | collective-permute-start | bytes 294920 | tf_op jit(solution)/shard_map/ppermute | solution.py:406
  (38 other events, 532.9 us)
